TPU v7x, 256 devices: a whole 4x4x8 slice. The times are simulated.
256 devices in a mesh: section: 8 (over x, core), vocab: 32 (over z, y).
Axes of the slice: x: 4, y: 4, z: 8, core: 2. Of those that a mesh axis runs over, the one named last changes fastest.
Arguments:
- hidden: bfloat16 [640, 8192], P('section')
- gain: float32 [4, 8192], replicated, may hold values from 0.5 to 1.5
- exit_scale: float32 [4], replicated, may hold values from 0.25 to 2
- head_weight: bfloat16 [8192, 65536], P(None, ('section', 'vocab'))
- targets: int32 [640], replicated, may hold values from 0 to 65535
- exit_ids: int32 [640], replicated, may hold values from 0 to 3
- counts: int32 [8], replicated, may hold values from 1 to 80, 512 in all
Outputs:
- loss: float32 [], replicated
- grad_weight: bfloat16 [8192, 65536], P(None, ('section', 'vocab'))
- grad_hidden: bfloat16 [640, 8192], P('section', 'vocab')
Inputs may be any that keep to these rules, and one draw needn't show every extreme that they name: Section s holds its live rows in its first counts[s] slots; the counts sum to 512 and some section holds exactly 80.
All inputs are finite; a program needn't handle non-finite values.
Results may differ from a plain program's by a relative error of at most 0.0085.
Values may be sent and summed in bfloat16 or wider, within the bound.
A program may use at most 128 MiB of HBM per device.

v0:
```python
import jax
import jax.numpy as jnp
from jax import lax
from jax.sharding import PartitionSpec as P

ROWS_SECTION = 64


def body(hidden, gain, exit_scale, head_weight, targets, exit_ids, counts):
    cap = hidden.shape[0]
    width = hidden.shape[1]
    voc_width = head_weight.shape[1]
    n_section = lax.axis_size("section")
    n_vocab = lax.axis_size("vocab")
    section_pos = lax.axis_index("section")
    total_rows = ROWS_SECTION * n_section
    pad_rows = cap * n_section
    exit_count = gain.shape[0]
    col_width = width // n_vocab
    xf = hidden.astype(jnp.float32)
    rinv = lax.rsqrt(jnp.mean(xf * xf, axis=1) + 1e-05)
    own_exit = lax.dynamic_slice_in_dim(exit_ids, section_pos * cap, cap)
    own_onehot = (own_exit[:, None] == jnp.arange(exit_count, dtype=jnp.int32)[None, :]).astype(
        jnp.float32
    )
    g_rows = jnp.dot(own_onehot, gain, precision=lax.Precision.HIGHEST)
    normed = (xf * rinv[:, None] * g_rows).astype(jnp.bfloat16)
    gathered = lax.all_gather(normed, "section", axis=0, tiled=True)
    slots = jnp.arange(pad_rows, dtype=jnp.int32)
    section_of = slots // cap
    slot_in = slots % cap
    section_match = section_of[:, None] == jnp.arange(n_section, dtype=jnp.int32)[None, :]
    count_row = jnp.sum(jnp.where(section_match, counts[None, :], 0), axis=1)
    valid = (slot_in < count_row).astype(jnp.float32)
    exit_match = exit_ids[:, None] == jnp.arange(exit_count, dtype=jnp.int32)[None, :]
    scale_row = jnp.sum(jnp.where(exit_match, exit_scale[None, :], jnp.float32(0.0)), axis=1)
    weight_row = valid * scale_row
    logits = jnp.dot(gathered, head_weight, preferred_element_type=jnp.float32)
    first_col = lax.axis_index(("section", "vocab")) * voc_width
    local_target = targets - first_col
    hit = (jnp.arange(voc_width, dtype=jnp.int32)[None, :] == local_target[:, None]).astype(
        jnp.float32
    )
    chosen_part = jnp.sum(hit * logits, axis=1)
    peak = lax.pmax(jnp.max(logits, axis=1), ("section", "vocab"))
    total, chosen = lax.psum(
        (jnp.sum(jnp.exp(logits - peak[:, None]), axis=1), chosen_part), ("section", "vocab")
    )
    lse = peak + jnp.log(total)
    loss = jnp.sum(weight_row * (lse - chosen)) / total_rows
    dlogits = (weight_row[:, None] * (jnp.exp(logits - lse[:, None]) - hit)).astype(jnp.bfloat16)
    grad_weight = lax.dot_general(
        gathered, dlogits, (((0,), (0,)), ((), ())), preferred_element_type=jnp.float32
    ).astype(jnp.bfloat16)
    features = lax.psum_scatter(
        lax.dot_general(
            head_weight, dlogits, (((1,), (1,)), ((), ())), preferred_element_type=jnp.float32
        ),
        "vocab",
        scatter_dimension=0,
        tiled=True,
    )
    owned = lax.psum_scatter(features, "section", scatter_dimension=1, tiled=True)
    dnormed = owned.T
    first_feature = lax.axis_index("vocab") * col_width
    x_cols = lax.dynamic_slice_in_dim(xf, first_feature, col_width, 1)
    g_cols = lax.dynamic_slice_in_dim(g_rows, first_feature, col_width, 1)
    unit = x_cols * rinv[:, None]
    scaled = g_cols * dnormed
    inner = lax.psum(jnp.sum(scaled * unit, axis=1), "vocab") / width
    grad_hidden = (rinv[:, None] * (scaled - unit * inner[:, None])).astype(jnp.bfloat16)
    return (loss, grad_weight, grad_hidden)


def solution(mesh):
    in_specs = (P("section", None), P(), P(), P(None, ("section", "vocab")), P(), P(), P())
    out_specs = (P(), P(None, ("section", "vocab")), P("section", "vocab"))
    return jax.shard_map(body, mesh=mesh, in_specs=in_specs, out_specs=out_specs, check_vma=False)
```

profile of v0, /device:TPU:2, one launch (start us, length us, event | category | flops | bytes accessed | tf_op | source)
XLA Modules:
  0.0 623.2 jit_solution(3994208506546969339)
XLA Ops:
  7.2 0.0 copy-start
  7.2 0.0 copy-start.2
  7.2 0.0 copy-start.4
  7.2 0.0 copy-start.5
  7.2 0.0 copy-start.3
  7.2 0.0 all-gather.2.cloned.1.call-start
  7.3 1.7 multiply_reduce_fusion
  9.0 0.8 dynamic_slice.9
  9.8 0.0 copy-done
  9.8 4.6 multiply_convert_fusion
  14.4 0.0 all-gather.2.cloned.1.call-update
  14.4 0.0 reduce-scatter.3.cloned.1.call-start
  14.5 0.0 copy-done.2
  14.5 0.1 select_reduce_fusion.2
  14.6 0.1 select_reduce_fusion.1
  14.7 63.2 %all-gather.2.cloned.1.call-done = bf16[640,8192]{1,0:T(8,128)(2,1)} async-done(((bf16[80,8192]{1,0:T(8,128)(2,1)}), bf16[640,8192]{1,0:T(8,128)(2,1)}) %all-gather.2.cloned.1.call-update) | async-done | bytes 10485776 | tf_op jit(solution)/shard_map/all_gather | solution.py:28
  77.9 11.0 %fusion.10 = (f32[640]{0:T(1024)S(1)}, f32[640,256]{0,1:T(8,128)S(1)}) fusion(bf16[640,8192]{1,0:T(8,128)(2,1)} %all-gather.2.cloned.1.call-done, bf16[8192,256]{1,0:T(8,128)(2,1)} %param.10), kind=kOutput, calls=%fused_computation.36 | convolution fusion | flops 2684517888 | bytes 15337984 | tf_op jit(solution)/shard_map/dot_general | solution.py:38
  88.9 76.7 %pmax.7 = f32[640]{0:T(1024)S(1)} all-reduce(f32[640]{0:T(1024)S(1)} %get-tuple-element.12), channel_id=1, replica_groups=mesh['section'=8,'vocab'=32] {'section','vocab'}, use_global_device_ids=true, to_apply=%region_4.5 | all-reduce | flops 640 | bytes 5120 | tf_op jit(solution)/shard_map/pmax | solution.py:45
  165.6 0.2 select_reduce_fusion
  165.8 74.3 %all-reduce = (f32[640]{0:T(1024)S(1)}, f32[640]{0:T(1024)S(1)}) all-reduce(f32[640]{0:T(1024)S(1)} %get-tuple-element.4, f32[640]{0:T(1024)S(1)} %get-tuple-element.3), channel_id=1, replica_groups=mesh['section'=8,'vocab'=32] {'section','vocab'}, use_global_device_ids=true, to_apply=%region_6.7 | all-reduce | flops 1280 | bytes 10240 | tf_op jit(solution)/shard_map/psum | solution.py:46
  240.1 0.6 multiply_reduce_fusion.2
  240.7 12.1 %convolution_bitcast_fusion = f32[8192,640]{0,1:T(8,128)} fusion(bf16[8192,256]{1,0:T(8,128)(2,1)} %param.10, f32[640,256]{0,1:T(8,128)S(1)} %get-tuple-element.13, f32[640]{0:T(1024)S(1)} %get-tuple-element.8, f32[640]{0:T(1024)S(1)} %get-tuple-element.9, s32[640]{0:T(1024)S(1)} %broadcast_subtract_fusion), kind=kOutput, calls=%fused_computation | convolution fusion | flops 2685337600 | bytes 25828864 | tf_op jit(solution)/shard_map/dot_general | solution.py:56
  252.8 0.0 reduce-scatter.3.cloned.1.call-update
  252.9 0.2 reduce-scatter.5.cloned.1.call-start
  253.1 252.9 %reduce-scatter.3.cloned.1.call-done = f32[256,640]{0,1:T(8,128)} async-done(((f32[8192,640]{0,1:T(8,128)}), f32[256,640]{0,1:T(8,128)}) %reduce-scatter.3.cloned.1.call-update) | async-done | bytes 655376 | tf_op jit(solution)/shard_map/reduce_scatter | solution.py:55
  506.0 0.0 reduce-scatter.5.cloned.1.call-update
  506.0 1.7 convert_element_type.20
  508.4 9.6 %convolution_convert_fusion = bf16[8192,256]{1,0:T(8,128)(2,1)} fusion(bf16[640,8192]{1,0:T(8,128)(2,1)} %all-gather.2.cloned.1.call-done, f32[640,256]{0,1:T(8,128)S(1)} %get-tuple-element.13, f32[640]{0:T(1024)S(1)} %get-tuple-element.8, f32[640]{0:T(1024)S(1)} %get-tuple-element.9, s32[640]{0:T(1024)S(1)} %broadcast_subtract_fusion), kind=kOutput, calls=%fused_computation.1 | convolution fusion | flops 2687434752 | bytes 15343104 | tf_op jit(solution)/shard_map/dot_general | solution.py:52
  518.0 19.6 %reduce-scatter.5.cloned.1.call-done = f32[256,80]{0,1:T(8,128)} async-done(((f32[256,640]{0,1:T(8,128)}), f32[256,80]{0,1:T(8,128)}) %reduce-scatter.5.cloned.1.call-update) | async-done | bytes 81936 | tf_op jit(solution)/shard_map/reduce_scatter | solution.py:63
  537.6 1.1 multiply_reduce_fusion.1
  538.8 75.1 %psum.23 = f32[80]{0:T(128)S(1)} all-reduce(f32[80]{0:T(128)S(1)} %multiply_reduce_fusion.1), channel_id=1, replica_groups=mesh['section'=8,'vocab'=32] {'vocab'}, use_global_device_ids=true, to_apply=%region_13.14 | all-reduce | flops 80 | bytes 640 | tf_op jit(solution)/shard_map/psum | solution.py:70
  613.8 1.7 multiply_convert_fusion.2
  (9 shorter events, 0.0 us)
Async XLA Ops:
  7.2 2.6 copy-start
  7.2 7.3 %copy-start.2 = (s32[640]{0:T(1024)S(1)}, s32[640]{0:T(1024)}, u32[]{:S(2)}) copy-start(s32[640]{0:T(1024)} %param.12) | copy-start | bytes 7684
  7.2 7.3 %copy-start.4 = (f32[4]{0:T(128)S(1)}, f32[4]{0:T(128)}, u32[]{:S(2)}) copy-start(f32[4]{0:T(128)} %param.9) | copy-start | bytes 52
  7.2 7.4 %copy-start.5 = (s32[8]{0:T(128)S(1)}, s32[8]{0:T(128)}, u32[]{:S(2)}) copy-start(s32[8]{0:T(128)} %param.13) | copy-start | bytes 100
  7.2 7.5 %copy-start.3 = (s32[640]{0:T(1024)S(1)}, s32[640]{0:T(1024)}, u32[]{:S(2)}) copy-start(s32[640]{0:T(1024)} %param.11) | copy-start | bytes 7684
  7.2 70.7 %all-gather.2.cloned.1.call-start = ((), (), s32[]{:S(2)}) async-start(), calls=%async_computation.2 | async-start | bytes 11796480 | tf_op jit(solution)/shard_map/all_gather | solution.py:28
  14.4 491.6 %reduce-scatter.3.cloned.1.call-start = ((), (), s32[]{:S(2)}) async-start(), calls=%async_computation.3 | async-start | bytes 21626880 | tf_op jit(solution)/shard_map/reduce_scatter | solution.py:55
  252.8 253.2 %copy-start.1 = (bf16[80,8192]{1,0:T(8,128)(2,1)S(1)}, bf16[80,8192]{1,0:T(8,128)(2,1)}, u32[]{:S(2)}) copy-start(bf16[80,8192]{1,0:T(8,128)(2,1)} %param.7) | copy-start | bytes 3932164
  252.9 284.7 %reduce-scatter.5.cloned.1.call-start = ((), (), s32[]{:S(2)}) async-start(), calls=%async_computation.4 | async-start | bytes 737280 | tf_op jit(solution)/shard_map/reduce_scatter | solution.py:63
Sparse Core Ops, SparseCore 0:
  14.5 63.3 all-gather.1
  253.0 252.9 reduce-scatter.2
  508.5 29.0 reduce-scatter.4
where the time goes:
time: 625 us; the launch traced here: 623 us
  waiting for transfers between devices  336 us (54%)
  blocking collectives  226 us (36%)
  matrix products  37.3 us (6%)
  between operations  15.7 us (3%)
  other arithmetic  7.2 us (1%)
    reduce_scatter x1, waiting for transfers between devices, body(): lax.psum_scatter(lax.dot_general(head_weight, dlogits, (((1,), (1,)), (()...  253 us
    pmax x1, blocking collectives, body(): peak = lax.pmax(jnp.max(logits, axis=1), ('section', 'vocab'))  76.7 us
    psum x1, blocking collectives, body(): inner = lax.psum(jnp.sum(scaled * unit, axis=1), 'vocab') / width  75.1 us
    psum x1, blocking collectives, body(): lax.psum((jnp.sum(jnp.exp(logits - peak[:, None]), axis=1), chosen_part),...  74.3 us
    all_gather x1, waiting for transfers between devices, body(): gathered = lax.all_gather(normed, 'section', axis=0, tiled=True)  63.2 us
    reduce_scatter x1, waiting for transfers between devices, body(): lax.psum_scatter(features, 'section', scatter_dimension=1, tiled=True)  19.6 us
  transfers between devices with their start and end apart: 3, of which 3 were waited for; matrix products, arithmetic and copies ran while one was open for 2% of the time, Pallas kernels for 0%

commit v1 on v0

v1 whole, which is shorter than its diff:
```python
import jax
import jax.numpy as jnp
from jax import lax
from jax.experimental import pallas as pl
from jax.experimental.pallas import tpu as pltpu
from jax.sharding import PartitionSpec as P

MESH = pl.DeviceIdType.MESH
NX, NZ, NY = 4, 8, 4
CAP = 80
D = 8192
VW = 256
ROWS = NX * CAP
EXITS = 4
F32 = jnp.float32
BF16 = jnp.bfloat16
ZW, YW = 384, 768
XB0, XA0 = NZ * ZW + NY * YW, NZ * ZW + NY * YW + 512
ZORD = (4, 3, 5, 2, 6, 1, 7, 0)
ZPOS = {d: k for k, d in enumerate(ZORD)}
N_SEM = 176


def kernel(
    hidden, gain, head, meta, counts, scale, loss_out, gw_out, gh_out,
    n_all, w_all, logit, dl, s1, s2, st, loss_x, px, pz, py,
    rx1a, rx1b, rx2a, rx2b, rz1a, rz1b, rz2a, rz2b, ry1a, ry1b, ry2a, ry2b,
    qx1, qx2, qz1, qz2, qy1, qy2, tx, tz, ty, dn, gs, gr, cols_f, ssem, rsem, lsem,
):
    s = lax.axis_index("section")
    v = lax.axis_index("vocab")
    x, c = lax.div(s, 2), lax.rem(s, 2)
    z, y = lax.div(v, NY), lax.rem(v, NY)

    def dev(dx=0, dc=0, dz=0, dy=0):
        return (
            lax.rem(x + dx + NX, NX) * 2 + lax.rem(c + dc, 2),
            lax.rem(z + dz + NZ, NZ) * NY + lax.rem(y + dy + NY, NY),
        )

    used = [0]
    started = []

    def send(src, dst, device):
        i = used[0]
        used[0] += 1
        cp = pltpu.make_async_remote_copy(
            src_ref=src, dst_ref=dst, send_sem=ssem.at[i], recv_sem=rsem.at[i],
            device_id=device, device_id_type=MESH,
        )
        cp.start()
        started.append(cp)
        return cp

    barrier = pltpu.get_barrier_semaphore()
    friends = [dict(dc=1)]
    friends += [dict(dz=i) for i in range(1, NZ)]
    friends += [dict(dx=i, dy=j) for i in range(NX) for j in range(NY) if i or j]
    for f in friends:
        pl.semaphore_signal(barrier, inc=1, device_id=dev(**f), device_id_type=MESH)
    own_w = pltpu.make_async_copy(head, w_all.at[c], lsem.at[0])
    own_w.start()

    diag = lax.broadcasted_iota(jnp.int32, (CAP, 128), 0) == lax.broadcasted_iota(
        jnp.int32, (CAP, 128), 1
    )
    lane = lax.broadcasted_iota(jnp.int32, (1, 128), 1)
    sub8 = lax.broadcasted_iota(jnp.int32, (8, 128), 0)

    def to_col(row):
        return jnp.sum(jnp.where(diag, jnp.broadcast_to(row, (CAP, 128)), 0.0), axis=1, keepdims=True)

    def to_row(col):
        return jnp.sum(jnp.where(diag, jnp.broadcast_to(col, (CAP, 128)), 0.0), axis=0, keepdims=True)

    own_exit = to_col(meta[1, pl.ds(s, 1), :].astype(F32))

    def gain_rows(cols, e):
        g = jnp.broadcast_to(gain[0:1, cols], (CAP, cols.size))
        for i in range(1, EXITS):
            g = jnp.where(e == float(i), gain[i : i + 1, cols], g)
        return g

    def squares(i, acc):
        xs = hidden[:, pl.ds(pl.multiple_of(i * 512, 512), 512)].astype(F32)
        xs = xs * xs
        for j in range(4):
            acc = acc + xs[:, j * 128 : (j + 1) * 128]
        return acc

    total = lax.fori_loop(0, D // 512, squares, jnp.zeros((CAP, 128), F32))
    rinv = lax.rsqrt(jnp.sum(total, axis=1, keepdims=True) / D + 1e-05)

    def norm_chunk(i, carry):
        cols = pl.ds(pl.multiple_of(i * 512, 512), 512)
        xs = hidden[:, cols].astype(F32)
        n_all[0, :, cols] = (xs * rinv * gain_rows(cols, own_exit)).astype(BF16)
        return carry

    lax.fori_loop(0, D // 512, norm_chunk, 0)

    pl.semaphore_wait(barrier, len(friends))

    def zc(d):
        return pl.ds(pl.multiple_of(lax.rem(z + d + NZ, NZ) * ZW, ZW), ZW)

    def yc(d):
        return pl.ds(pl.multiple_of(NZ * ZW + lax.rem(y + d + NY, NY) * YW, YW), YW)

    xb, xa = pl.ds(XB0, 512), pl.ds(XA0, D - XA0)
    low, high, full = pl.ds(0, 48), pl.ds(48, 32), pl.ds(0, CAP)
    events = []
    cps = {}

    def at(time, fn):
        events.append((time, len(events), fn))

    def run():
        for _, _, fn in sorted(events, key=lambda e: (e[0], e[1])):
            fn()
        events.clear()

    def own_x(tag, cols):
        cps[tag + "+"] = send(n_all.at[0, :, cols], n_all.at[3, :, cols], dev(dx=1))
        cps[tag + "-"] = send(n_all.at[0, :, cols], n_all.at[1, :, cols], dev(dx=-1))

    def forward_x(tag, cols, right):
        if right:
            cps[tag + "2"] = send(n_all.at[3, :, cols], n_all.at[2, :, cols], dev(dx=1))
        else:
            cps[tag + "2"] = send(n_all.at[1, :, cols], n_all.at[2, :, cols], dev(dx=-1))

    def chain(tag, n, cols, axis, rel, t0, step):
        half = n // 2

        def begin():
            for sign in (1, -1):
                ref = n_all.at[rel, :, cols(0)]
                cps[tag, sign, 1] = send(ref, ref, dev(**{axis: sign}))

        def arrive(sign, k):
            cps[tag, sign, k].wait_recv()
            if k < half:
                rows = full if k < half - 1 else (low if sign == 1 else high)
                ref = n_all.at[rel, rows, cols(-sign * k)]
                cps[tag, sign, k + 1] = send(ref, ref, dev(**{axis: sign}))

        for k in range(1, half + 1):
            for sign in (1, -1):
                at(t0 + step * k, lambda sign=sign, k=k: arrive(sign, k))
        return begin

    own_x("z", zc(0))
    own_x("y", yc(0))
    z1 = chain("z1", NZ, zc, "dz", 1, 3.0, 4.0)
    z3 = chain("z3", NZ, zc, "dz", 3, 3.5, 4.0)
    z2 = chain("z2", NZ, zc, "dz", 2, 5.5, 4.0)
    y1 = chain("y1", NY, yc, "dy", 1, 5.0, 5.2)
    y3 = chain("y3", NY, yc, "dy", 3, 5.5, 5.2)
    y2 = chain("y2", NY, yc, "dy", 2, 8.0, 5.2)

    def got(tag, sign, then):
        def fn():
            cps[tag + sign].wait_recv()
            then()
        return fn

    def ready_z1():
        z1()
        forward_x("z", zc(0), False)
        own_x("a", xa)
        own_x("b", xb)

    def ready_y1():
        y1()
        forward_x("y", yc(0), False)

    at(3.0, got("z", "-", ready_z1))
    at(3.1, got("z", "+", z3))
    at(5.0, got("y", "-", ready_y1))
    at(5.1, got("y", "+", y3))
    at(5.5, got("z", "2", z2))
    at(8.0, got("y", "2", y2))
    at(11.0, got("b", "-", lambda: forward_x("b", xb, False)))
    at(11.1, got("b", "+", lambda: None))
    at(12.0, got("a", "+", lambda: forward_x("a", xa, True)))
    at(12.1, got("a", "-", lambda: None))
    at(16.0, got("b", "2", lambda: None))
    at(18.0, got("a", "2", lambda: None))

    def swap_w():
        own_w.wait()
        cps["w"] = send(w_all.at[c], w_all.at[c], dev(dc=1))

    at(3.2, swap_w)
    run()
    cps["w"].wait_recv()

    def logit_chunk(i, carry):
        k = pl.multiple_of(i * 512, 512)
        n = n_all[:, :, pl.ds(k, 512)].reshape(ROWS, 512)
        for h in range(2):
            part = jnp.dot(n, w_all[h, pl.ds(k, 512), :], preferred_element_type=F32)
            logit[h] += part
        return carry

    logit[...] = jnp.zeros_like(logit)
    lax.fori_loop(0, D // 512, logit_chunk, 0)

    def section_of(rel):
        return lax.rem(x + rel, NX) * 2 + c

    def first_entry(h):
        return (((x * 2 + h) * NZ * NY + v) * VW).astype(F32)

    entry = lax.broadcasted_iota(jnp.int32, (CAP, VW), 1).astype(F32)

    def hits(rel, h):
        target = to_col(meta[0, pl.ds(section_of(rel), 1), :].astype(F32))
        return entry == target - first_entry(h)

    stats = [jnp.zeros((8, 128), F32)] * 4
    for rel in range(NX):
        rows = pl.ds(rel * CAP, CAP)
        part = [logit[h, rows, :] for h in range(2)]
        m = jnp.maximum(*[jnp.max(l, axis=1, keepdims=True) for l in part])
        e = [jnp.exp(l - m) for l in part]
        values = (
            m,
            sum(jnp.sum(p, axis=1, keepdims=True) for p in e),
            sum(jnp.sum(p * l, axis=1, keepdims=True) for p, l in zip(e, part)),
            sum(
                jnp.sum(jnp.where(hits(rel, h), l, 0.0), axis=1, keepdims=True)
                for h, l in enumerate(part)
            ),
        )
        here = sub8 == lax.rem(x + rel, NX)
        for i in range(4):
            stats[i] = jnp.where(here, jnp.broadcast_to(to_row(values[i]), (8, 128)), stats[i])

    def merge(parts):
        peak = parts[0][0]
        for p in parts[1:]:
            peak = jnp.maximum(peak, p[0])
        f = [jnp.exp(p[0] - peak) for p in parts]
        return (
            peak,
            sum(p[1] * g for p, g in zip(parts, f)),
            sum(p[2] * g for p, g in zip(parts, f)),
            sum(p[3] for p in parts),
        )

    for i in range(4):
        s1[z, i] = stats[i]
    swaps = [send(s1.at[z], s1.at[z], dev(dz=i)) for i in range(1, NZ)]
    for cp in swaps:
        cp.wait_recv()
    stats = merge([[s1[q, i] for i in range(4)] for q in range(NZ)])
    own = x * NY + y
    for i in range(4):
        s2[own, i] = stats[i]
    swaps = [
        send(s2.at[own], s2.at[own], dev(dx=i, dy=j))
        for i in range(NX) for j in range(NY) if i or j
    ]
    for cp in swaps:
        cp.wait_recv()
    peak, total, mean, chosen = merge([[s2[q, i] for i in range(4)] for q in range(NX * NY)])
    lse = peak + jnp.log(total)

    weight = jnp.zeros((8, 128), F32)
    for q in range(NX):
        sec = q * 2 + c
        ids = meta[1, pl.ds(sec, 1), :]
        w_row = jnp.zeros((1, 128), F32)
        for i in range(EXITS):
            w_row = jnp.where(ids == i, scale[i], w_row)
        w_row = jnp.where(lane < counts[sec], w_row, 0.0)
        weight = jnp.where(sub8 == q, jnp.broadcast_to(w_row, (8, 128)), weight)
    live = weight != 0.0
    st[0] = lse
    st[1] = weight
    st[2] = jnp.where(live, weight * (mean / total - chosen), 0.0)
    loss_rows = jnp.where(live, weight * (lse - chosen), 0.0)
    own_loss = jnp.sum(jnp.sum(loss_rows, axis=1, keepdims=True), axis=0, keepdims=True)
    loss_x[0] = jnp.broadcast_to(own_loss, (8, 128))
    loss_swap = send(loss_x.at[0], loss_x.at[1], dev(dc=1))

    for rel in range(NX):
        rows = pl.ds(rel * CAP, CAP)
        at_row = pl.ds(lax.rem(x + rel, NX), 1)
        lse_c, w_c = to_col(st[0, at_row, :]), to_col(st[1, at_row, :])
        for h in range(2):
            hit = jnp.where(hits(rel, h), 1.0, 0.0)
            dl[h, rows, :] = (w_c * (jnp.exp(logit[h, rows, :] - lse_c) - hit)).astype(BF16)

    nt = (((1,), (1,)), ((), ()))

    def grad_block(k):
        zz = lax.rem(z + ZORD[k], NZ)

        def one(ry, carry):
            at_f = pl.ds(pl.multiple_of((zz * NY + lax.rem(y + ry, NY)) * VW, VW), VW)
            out = lax.dot_general(dl[0], w_all[0, at_f, :], nt, preferred_element_type=F32)
            out += lax.dot_general(dl[1], w_all[1, at_f, :], nt, preferred_element_type=F32)
            out = out.astype(BF16)
            for rx in range(NX):
                px[rx, k, ry] = out[rx * CAP : rx * CAP + 32]
                pz[k, rx, ry] = out[rx * CAP + 32 : rx * CAP + 64]
                py[ry, rx, k] = out[rx * CAP + 64 : rx * CAP + 80]
            return carry

        lax.fori_loop(0, NY, one, 0)

    def add_into(dst, srcs):
        def one(i, carry):
            acc = dst[i].astype(F32)
            for r in srcs:
                acc = acc + r[i].astype(F32)
            dst[i] = acc.astype(BF16)
            return carry

        lax.fori_loop(0, dst.shape[0], one, 0)

    def ring(tag, n, axis, block, halves, bufs, times, done):
        half = n // 2
        h_a, h_b = halves

        def begin(sign):
            src = h_a(block(half)) if sign == 1 else h_b(block(half))
            cps[tag, sign, 1] = send(src, bufs[sign][0], dev(**{axis: sign}))

        def arrive(sign, k):
            cps[tag, sign, k].wait_recv()
            d = (sign * (half - k)) % n
            if k == 1:
                part = h_a(block(d)) if sign == 1 else h_b(block(d))
                add_into(part, [bufs[sign][0]])
            else:
                add_into(block(d), [bufs[sign][1].at[k - 2]])
            cps[tag, sign, k + 1] = send(block(d), bufs[sign][1].at[k - 1], dev(**{axis: sign}))

        def finish():
            for sign in (1, -1):
                cps[tag, sign, half].wait_recv()
            add_into(block(0), [bufs[sign][1].at[half - 2] for sign in (1, -1)])
            done()

        for k in range(1, half):
            for sign in (1, -1):
                at(times[k - 1], lambda sign=sign, k=k: arrive(sign, k))
        at(times[half - 1], finish)
        return begin

    def direct(tag, n, axis, block, buf, time, done):
        def begin():
            for d in range(1, n):
                cps[tag, d] = send(block(d), buf.at[d - 1], dev(**{axis: d}))

        def finish():
            for d in range(1, n):
                cps[tag, d].wait_recv()
            acc = block(0)[...].astype(F32)
            for d in range(1, n):
                acc = acc + buf[d - 1].astype(F32)
            done(acc)

        at(time, finish)
        return begin

    def first(m):
        return lambda r: r.at[0:m]

    def last(m):
        return lambda r: r.at[m : 2 * m]

    def put(r0, r1):
        def fn(acc):
            dn[r0:r1] = acc
        return fn

    both = lambda begin: lambda: (begin(1), begin(-1))
    x3 = direct("x3", NZ, "dz", lambda d: px.at[0, ZPOS[d], 0], tx, 28.0, put(0, 32))
    x2 = ring("x2", NY, "dy", lambda d: px.at[0, :, d], (first(4), last(4)),
              {1: (qx1.at[0], rx2a), -1: (qx1.at[1], rx2b)}, (20.0, 22.5), x3)
    x1 = ring("x1", NX, "dx", lambda d: px.at[d], (first(4), last(4)),
              {1: (rx1a, qx2.at[0:1]), -1: (rx1b, qx2.at[1:2])}, (7.0, 17.5), both(x2))
    z3r = direct("w3", NY, "dy", lambda d: pz.at[7, 0, d], tz, 28.1, put(32, 64))
    z2r = ring("w2", NX, "dx", lambda d: pz.at[7, d], (first(2), last(2)),
               {1: (qz1.at[0], rz2a), -1: (qz1.at[1], rz2b)}, (22.0, 24.5), z3r)
    z1r = ring("w1", NZ, "dz", lambda d: pz.at[ZPOS[d]], (first(2), last(2)),
               {1: (rz1a, qz2.at[0]), -1: (rz1b, qz2.at[1])}, (3.5, 9.0, 14.5, 20.0), both(z2r))
    y3r = direct("v3", NX, "dx", lambda d: py.at[0, d, 7], ty, 24.0, put(64, 80))
    y2r = ring("v2", NZ, "dz", lambda d: py.at[0, :, ZPOS[d]], (first(2), last(2)),
               {1: (qy1.at[0], ry2a), -1: (qy1.at[1], ry2b)}, (12.5, 14.6, 16.5, 18.5), y3r)
    y1r = ring("v1", NY, "dy", lambda d: py.at[d], (first(2), last(2)),
               {1: (ry1a, qy2.at[0:1]), -1: (ry1b, qy2.at[1:2])}, (5.0, 10.5), both(y2r))

    tn = (((0,), (0,)), ((), ()))

    def head_rows(j, h, store):
        def one(i, carry):
            f = pl.ds(pl.multiple_of(j * 1024 + i * VW, VW), VW)
            n = n_all[:, :, f].reshape(ROWS, VW)
            store(f, lax.dot_general(n, dl[h], tn, preferred_element_type=F32))
            return carry

        lax.fori_loop(0, 4, one, 0)

    def partner_chunk(j):
        def store(f, value):
            gs[f, :] = value.astype(BF16)

        head_rows(j, 1 - c, store)
        f = pl.ds(j * 1024, 1024)
        cps["g", j] = send(gs.at[f], gr.at[f], dev(dc=1))

    outs = []

    def own_chunk(j):
        cps["g", j].wait_recv()

        def store(f, value):
            gr[f, :] = (value + gr[f, :].astype(F32)).astype(BF16)

        head_rows(j, c, store)
        f = pl.ds(j * 1024, 1024)
        cp = pltpu.make_async_copy(gr.at[f], gw_out.at[f], lsem.at[1 + j])
        cp.start()
        outs.append(cp)

    for j in range(8):
        at(4.0 + j * 1.0, lambda j=j: partner_chunk(j))
        at(12.1 + j * 1.0, lambda j=j: own_chunk(j))

    grad_block(0)
    z1r(1)
    z1r(-1)
    for k in range(1, 4):
        grad_block(k)
    x1(1)
    for k in range(4, 8):
        grad_block(k)
    x1(-1)
    y1r(1)
    y1r(-1)
    run()

    f = pl.ds(pl.multiple_of(v * VW, VW), VW)
    inner = to_col(st[2, pl.ds(x, 1), :])
    unit = hidden[:, f].astype(F32) * rinv
    scaled = gain_rows(f, own_exit) * dn[...]
    gh_out[...] = (rinv * (scaled - unit * (inner / D))).astype(BF16)

    loss_swap.wait_recv()
    loss_out[...] = (loss_x[0, 0:1, 0:1] + loss_x[1, 0:1, 0:1]) / 512.0
    for cp in outs:
        cp.wait()
    for cp in started:
        cp.wait_send()


def body(hidden, gain, exit_scale, head_weight, targets, exit_ids, counts):
    meta = jnp.stack([targets, exit_ids]).reshape(2, 2 * NX, CAP)
    meta = jnp.pad(meta, ((0, 0), (0, 0), (0, 128 - CAP)))
    vmem = pl.BlockSpec(memory_space=pltpu.VMEM)
    smem = pl.BlockSpec(memory_space=pltpu.SMEM)
    hbm = pl.BlockSpec(memory_space=pl.ANY)
    b = lambda *shape: pltpu.VMEM(shape, BF16)
    f = lambda *shape: pltpu.VMEM(shape, F32)
    scratch = [
        b(NX, CAP, D), b(2, D, VW), f(2, ROWS, VW), b(2, ROWS, VW),
        f(NZ, 4, 8, 128), f(NX * NY, 4, 8, 128), f(3, 8, 128), f(2, 8, 128),
        b(NX, NZ, NY, 32, VW), b(NZ, NX, NY, 32, VW), b(NY, NX, NZ, 16, VW),
        b(4, NY, 32, VW), b(4, NY, 32, VW), b(1, NZ, 32, VW), b(1, NZ, 32, VW),
        b(2, NY, 32, VW), b(2, NY, 32, VW), b(1, NY, 32, VW), b(1, NY, 32, VW),
        b(2, NZ, 16, VW), b(2, NZ, 16, VW), b(3, NX, 16, VW), b(3, NX, 16, VW),
        b(2, 4, 32, VW), b(2, NZ, NY, 32, VW),
        b(2, 2, 32, VW), b(2, 3, NX, NY, 32, VW),
        b(2, 2, 16, VW), b(2, NX, NZ, 16, VW),
        b(NZ - 1, 32, VW), b(NY - 1, 32, VW), b(NX - 1, 16, VW),
        f(CAP, VW), b(D, VW), b(D, VW), f(8, 128),
        pltpu.SemaphoreType.DMA((N_SEM,)), pltpu.SemaphoreType.DMA((N_SEM,)),
        pltpu.SemaphoreType.DMA((9,)),
    ]
    loss, grad_weight, grad_hidden = pl.pallas_call(
        kernel,
        out_shape=(
            jax.ShapeDtypeStruct((1, 1), F32),
            jax.ShapeDtypeStruct((D, VW), BF16),
            jax.ShapeDtypeStruct((CAP, VW), BF16),
        ),
        in_specs=[vmem, vmem, hbm, vmem, smem, smem],
        out_specs=(vmem, hbm, vmem),
        scratch_shapes=scratch,
        compiler_params=pltpu.CompilerParams(
            collective_id=0, has_side_effects=True, vmem_limit_bytes=58 * 2**20
        ),
        name="exit_head",
    )(hidden, gain, head_weight, meta, counts, exit_scale)
    return (loss[0, 0], grad_weight, grad_hidden)


def solution(mesh):
    in_specs = (P("section", None), P(), P(), P(None, ("section", "vocab")), P(), P(), P())
    out_specs = (P(), P(None, ("section", "vocab")), P("section", "vocab"))
    return jax.shard_map(body, mesh=mesh, in_specs=in_specs, out_specs=out_specs, check_vma=False)
```

time: 625 us -> 124 us (0.20)
  waiting for transfers between devices: 336 us -> 0 us
  blocking collectives: 226 us -> 0 us
  Pallas kernels: 0 us -> 114 us
  matrix products: 37.3 us -> 0 us
  between operations: 15.7 us -> 2.46 us
  other arithmetic: 7.2 us -> 0.01 us
  local copies, waits for them, and re-layouts: 0.8 us -> 7.23 us
    reduce_scatter x2 -> x0, waiting for transfers between devices: 273 us -> none  [the longest x1 253 us: body(): lax.psum_scatter(lax.dot_general(head_weight, dlogits, (((1,), (1,)), (()...]
    psum x2 -> x0, blocking collectives: 149 us -> none  [the longest x1 75.1 us: body(): inner = lax.psum(jnp.sum(scaled * unit, axis=1), 'vocab') / width]
    pallas_call x0 -> x1, Pallas kernels: none -> 114 us  [body(): pl.pallas_call(kernel, out_shape=(jax.ShapeDtypeStruct((1, 1), F32), jax....]
    pmax x1 -> x0, blocking collectives: 76.7 us -> none  [body(): peak = lax.pmax(jnp.max(logits, axis=1), ('section', 'vocab'))]
    all_gather x1 -> x0, waiting for transfers between devices: 63.2 us -> none  [body(): gathered = lax.all_gather(normed, 'section', axis=0, tiled=True)]
    dot_general x4 -> x0, matrix products: 37.3 us -> none  [the longest x1 12.1 us: body(): lax.dot_general(head_weight, dlogits, (((1,), (1,)), ((), ())), preferred...]
  transfers between devices with their start and end apart: 3 -> 0, of which waited for: 3 -> 0; matrix products, arithmetic and copies ran while one was open for 2% -> 0% of each run, Pallas kernels for 0% -> 0%
where the time goes in v1:
time: 124 us
  Pallas kernels  114 us (92%)
  local copies, waits for them, and re-layouts  7.23 us (6%)
  between operations  2.46 us (2%)
    pallas_call x1, Pallas kernels, body(): pl.pallas_call(kernel, out_shape=(jax.ShapeDtypeStruct((1, 1), F32), jax....  114 us
    unnamed x4, local copies, waits for them, and re-layouts  5.1 us

profile of v1, /device:TPU:2, one launch (start us, length us, event | category | flops | bytes accessed | tf_op | source)
XLA Modules:
  0.0 124.1 jit_solution(10379917666669902413)
XLA Ops:
  0.6 0.8 stack.9
  1.4 0.8 stack.10
  2.2 0.6 pad.4.meta
  2.8 114.4 %exit_head.1 = (f32[1,1]{1,0:T(1,128)}, bf16[8192,256]{1,0:T(8,128)(2,1)}, bf16[80,256]{1,0:T(8,128)(2,1)}) custom-call(bf16[80,8192]{1,0:T(8,128)(2,1)} %hidden.1, f32[4,8192]{1,0:T(4,128)} %gain.1, bf16[8192,256]{1,0:T(8,128)(2,1)} %head.1, s32[2,8,128]{2,1,0:T(8,128)} %pad.4.meta, s32[8]{0:T(128)} %counts.1, f32[4]{0:T(128)} %scale.1), custom_call_target="tpu_custom_call" | custom-call | tf_op jit(solution)/shard_map/exit_head/pallas_call | solution.py:486
  117.8 0.0 copy-start
  117.9 4.5 %copy.14 = bf16[8192,256]{1,0:T(8,128)(2,1)} copy(bf16[8192,256]{1,0:T(8,128)(2,1)} %get-tuple-element.13) | data formatting | bytes 8388608
  122.3 0.0 copy-done
  122.3 0.6 copy.15
  (1 shorter events, 0.0 us)
Async XLA Ops:
  117.8 4.5 %copy-start = (bf16[80,256]{1,0:T(8,128)(2,1)S(1)}, bf16[80,256]{1,0:T(8,128)(2,1)}, u32[]{:S(2)}) copy-start(bf16[80,256]{1,0:T(8,128)(2,1)} %get-tuple-element.14) | copy-start | bytes 122884

commit v2 on v0

v2 whole, which is shorter than its diff:
```python
import jax
import jax.numpy as jnp
from jax import lax
from jax.experimental import pallas as pl
from jax.experimental.pallas import tpu as pltpu
from jax.sharding import PartitionSpec as P

MESH = pl.DeviceIdType.MESH
NX, NZ, NY = 4, 8, 4
CAP = 80
D = 8192
VW = 256
ROWS = NX * CAP
EXITS = 4
F32 = jnp.float32
BF16 = jnp.bfloat16
ZW, YW = 384, 768
XB0 = NZ * ZW + NY * YW
XBW = 512
XA0 = XB0 + XBW
ZORD = (4, 3, 5, 2, 6, 1, 7, 0)
ZPOS = {d: k for k, d in enumerate(ZORD)}
N_SEM = 320
HALVES = ((0, 48, 32), (48, 32, 16))
PARTS = (((0, 0, 256), (16, 0, 256), (32, 0, 256)), ((48, 0, 256), (64, 0, 128), (64, 128, 128)))
NT = (((1,), (1,)), ((), ()))
TN = (((0,), (0,)), ((), ()))


def scratch():
    out = dict(
        hid=((CAP, D), BF16), gain=((EXITS, D), F32), n_all=((NX, CAP, D), BF16), w_all=((D, 2 * VW), BF16),
        logit=((NX, CAP, 2 * VW), F32), dl=((NX, CAP, 2 * VW), BF16),
        s1=((2, NZ, 4, 8, 128), F32), s2=((2, NX * NY, 4, 8, 128), F32),
        st=((2, 3, 8, 128), F32), ids=((2, 8, 128), F32), loss=((2, 8, 128), F32), dn=((CAP, VW), F32),
        mine=((D, VW), F32), gs=((D, VW), BF16), gr=((D, VW), BF16),
    )
    for h in range(2):
        lx, lz, ly = [p[2] for p in PARTS[h]]
        out[f"px{h}"] = ((NX, NZ, NY, 16, lx), BF16)
        out[f"pz{h}"] = ((NZ, NX, NY, 16, lz), BF16)
        out[f"py{h}"] = ((NY, NX, NZ, 16, ly), BF16)
        out[f"ax{h}"] = ((2, 2, 4, 2, 16, lx), BF16)
        out[f"bx{h}"] = ((2, 2, 1, NZ, 2, 16, lx), BF16)
        out[f"az{h}"] = ((2, 2, 2, 2, 16, lz), BF16)
        out[f"bz{h}"] = ((2, 2, 3, NX, 2, 16, lz), BF16)
        out[f"ay{h}"] = ((2, 2, 2, 4, 16, ly), BF16)
        out[f"by{h}"] = ((2, 2, 1, NX, 4, 16, ly), BF16)
        out[f"cx{h}"] = ((NY - 1, NZ, 16, lx), BF16)
        out[f"cz{h}"] = ((NX - 1, NY, 16, lz), BF16)
        out[f"cy{h}"] = ((NX - 1, NZ, 16, ly), BF16)
        out[f"ex{h}"] = ((NZ - 1, 16, lx), BF16)
        out[f"ez{h}"] = ((NY - 1, 16, lz), BF16)
        out[f"ey{h}"] = ((NZ - 1, 16, ly), BF16)
    return out


SCRATCH = scratch()


def kernel(hidden, gain_in, head, targets, exit_ids, counts, scale, loss_out, gw_out, gh_out, *refs):
    b = dict(zip(SCRATCH, refs))
    ssem, rsem, lsem = refs[len(SCRATCH) :]
    hid, gain, n_all, w_all = b["hid"], b["gain"], b["n_all"], b["w_all"]
    logit, dl, s1, s2, st, ids = b["logit"], b["dl"], b["s1"], b["s2"], b["st"], b["ids"]
    dn, mine, gs, gr, loss_x = b["dn"], b["mine"], b["gs"], b["gr"], b["loss"]
    s = lax.axis_index("section")
    v = lax.axis_index("vocab")
    x, c = lax.div(s, 2), lax.rem(s, 2)
    z, y = lax.div(v, NY), lax.rem(v, NY)

    def dev(dx=0, dc=0, dz=0, dy=0):
        return (
            lax.rem(x + dx + NX, NX) * 2 + lax.rem(c + dc, 2),
            lax.rem(z + dz + NZ, NZ) * NY + lax.rem(y + dy + NY, NY),
        )

    used = [0]
    started = []
    outs = []
    cps = {}
    events = []

    def send(src, dst, device):
        i = used[0]
        used[0] += 1
        cp = pltpu.make_async_remote_copy(
            src_ref=src, dst_ref=dst, send_sem=ssem.at[i], recv_sem=rsem.at[i],
            device_id=device, device_id_type=MESH,
        )
        cp.start()
        started.append(cp)
        return cp

    def at(time, fn, *args):
        events.append((time, len(events), lambda: fn(*args)))

    def run():
        for _, _, fn in sorted(events, key=lambda e: (e[0], e[1])):
            fn()
        events.clear()

    barrier = pltpu.get_barrier_semaphore()
    friends = [dict(dc=1)]
    friends += [dict(dz=i) for i in range(1, NZ)]
    friends += [dict(dx=i, dy=j) for i in range(NX) for j in range(NY) if i or j]
    for f in friends:
        pl.semaphore_signal(barrier, inc=1, device_id=dev(**f), device_id_type=MESH)
    own_w = pl.ds(pl.multiple_of(c * VW, VW), VW)
    loads = [
        pltpu.make_async_copy(hidden, hid, lsem.at[0]),
        pltpu.make_async_copy(gain_in, gain, lsem.at[1]),
        pltpu.make_async_copy(head, w_all.at[:, own_w], lsem.at[2]),
    ]
    for cp in loads:
        cp.start()

    diag = lax.broadcasted_iota(jnp.int32, (CAP, 128), 0) == lax.broadcasted_iota(
        jnp.int32, (CAP, 128), 1
    )
    lane = lax.broadcasted_iota(jnp.int32, (8, 128), 1)
    sub8 = lax.broadcasted_iota(jnp.int32, (8, 128), 0)
    flat = sub8 * 128 + lane

    def to_col(row):
        return jnp.sum(jnp.where(diag, jnp.broadcast_to(row, (CAP, 128)), 0.0), axis=1, keepdims=True)

    def to_row(col, r0):
        n = col.shape[0]
        return jnp.sum(
            jnp.where(diag[r0 : r0 + n], jnp.broadcast_to(col, (n, 128)), 0.0), axis=0, keepdims=True
        )

    def spread(slot, ref):
        def one(r, acc):
            for q in range(NX):
                acc = jnp.where(flat == q * 128 + r, ref[(q * 2 + c) * CAP + r], acc)
            return acc

        acc = lax.fori_loop(0, CAP, one, jnp.zeros((8, 128), jnp.int32), unroll=4)
        ids[slot] = acc.astype(F32)

    spread(0, exit_ids)
    own_exit = to_col(ids[0, pl.ds(x, 1), :])

    def gain_rows(cols, e):
        g = jnp.broadcast_to(gain[0:1, cols], (CAP, cols.size))
        for i in range(1, EXITS):
            g = jnp.where(e == float(i), gain[i : i + 1, cols], g)
        return g

    def squares(i, acc):
        xs = hid[:, pl.ds(pl.multiple_of(i * 512, 512), 512)].astype(F32)
        xs = xs * xs
        for j in range(4):
            acc = acc + xs[:, j * 128 : (j + 1) * 128]
        return acc

    loads[0].wait()
    total_sq = lax.fori_loop(0, D // 512, squares, jnp.zeros((CAP, 128), F32))
    rinv = lax.rsqrt(jnp.sum(total_sq, axis=1, keepdims=True) / D + 1e-05)

    def norm_chunk(i, carry):
        cols = pl.ds(pl.multiple_of(i * 512, 512), 512)
        xs = hid[:, cols].astype(F32)
        n_all[0, :, cols] = (xs * rinv * gain_rows(cols, own_exit)).astype(BF16)
        return carry

    loads[1].wait()
    lax.fori_loop(0, D // 512, norm_chunk, 0)
    pl.semaphore_wait(barrier, len(friends))

    def zc(d):
        return pl.ds(pl.multiple_of(lax.rem(z + d + NZ, NZ) * ZW, ZW), ZW)

    def yc(d):
        return pl.ds(pl.multiple_of(NZ * ZW + lax.rem(y + d + NY, NY) * YW, YW), YW)

    xb, xa = pl.ds(XB0, XBW), pl.ds(XA0, D - XA0)

    def own_x(tag, h, cols):
        rows = pl.ds(*HALVES[h][:2])
        cps[tag, h, 1] = send(n_all.at[0, rows, cols], n_all.at[3, rows, cols], dev(dx=1))
        cps[tag, h, -1] = send(n_all.at[0, rows, cols], n_all.at[1, rows, cols], dev(dx=-1))

    def forward_x(tag, h, cols, right):
        rows = pl.ds(*HALVES[h][:2])
        rel, dx = (3, 1) if right else (1, -1)
        cps[tag, h, 2] = send(n_all.at[rel, rows, cols], n_all.at[2, rows, cols], dev(dx=dx))

    def chain(tag, h, n, cols, axis, rel, t0, step):
        half = n // 2
        r0, n_rows, n_low = HALVES[h]
        full, low, high = pl.ds(r0, n_rows), pl.ds(r0, n_low), pl.ds(r0 + n_low, n_rows - n_low)

        def begin():
            for sign in (1, -1):
                ref = n_all.at[rel, full, cols(0)]
                cps[tag, h, rel, sign, 1] = send(ref, ref, dev(**{axis: sign}))

        def arrive(sign, k):
            cps[tag, h, rel, sign, k].wait_recv()
            if k < half:
                rows = full if k < half - 1 else (low if sign == 1 else high)
                ref = n_all.at[rel, rows, cols(-sign * k)]
                cps[tag, h, rel, sign, k + 1] = send(ref, ref, dev(**{axis: sign}))

        for k in range(1, half + 1):
            for sign in (1, -1):
                at(t0 + step * k, arrive, sign, k)
        return begin

    def gather(h, tz, ty, tb, ta, dz, dy, fwd, zstep, ystep, more):
        z1 = chain("cz", h, NZ, zc, "dz", 1, tz, zstep)
        z3 = chain("cz", h, NZ, zc, "dz", 3, tz + 0.1, zstep)
        z2 = chain("cz", h, NZ, zc, "dz", 2, tz + dz, zstep)
        y1 = chain("cy", h, NY, yc, "dy", 1, ty, ystep)
        y3 = chain("cy", h, NY, yc, "dy", 3, ty + 0.1, ystep)
        y2 = chain("cy", h, NY, yc, "dy", 2, ty + dy, ystep)

        def got(tag, sign, *then):
            cps[tag, h, sign].wait_recv()
            for fn in then:
                fn()

        at(tz, got, "z", -1, z1, lambda: forward_x("z", h, zc(0), False))
        at(tz, got, "z", 1, z3, *more)
        at(tz + dz, got, "z", 2, z2)
        at(ty, got, "y", -1, y1, lambda: forward_x("y", h, yc(0), False))
        at(ty, got, "y", 1, y3)
        at(ty + dy, got, "y", 2, y2)
        at(tb, got, "b", -1, lambda: forward_x("b", h, xb, False))
        at(tb, got, "b", 1)
        at(ta, got, "a", 1, lambda: forward_x("a", h, xa, True))
        at(ta, got, "a", -1)
        at(tb + fwd, got, "b", 2)
        at(ta + fwd, got, "a", 2)
        return max(e[0] for e in events) + 0.01

    def own_group(h):
        own_x("b", h, xb)
        own_x("a", h, xa)

    for h in range(2):
        own_x("z", h, zc(0))
        own_x("y", h, yc(0))

    here0 = gather(0, 3.0, 4.5, 7.0, 9.0, 1.6, 2.2, 4.0, 3.0, 4.0, (lambda: own_group(0),))
    here1 = gather(1, 4.6, 6.5, 12.0, 14.0, 1.6, 2.2, 4.0, 3.6, 4.6, (lambda: own_group(1),))

    def swap_w():
        loads[2].wait()
        cps["w"] = send(w_all.at[:, own_w], w_all.at[:, own_w], dev(dc=1))

    at(3.2, swap_w)
    at(3.3, spread, 1, targets)

    def weights():
        weight = jnp.zeros((8, 128), F32)
        exits = ids[0]
        for i in range(EXITS):
            weight = jnp.where(exits == float(i), scale[i], weight)
        for q in range(NX):
            weight = jnp.where((sub8 == q) & (lane >= counts[q * 2 + c]), 0.0, weight)
        for h in range(2):
            r0, n_rows, _ = HALVES[h]
            st[h, 1] = jnp.where((sub8 < NX) & (lane >= r0) & (lane < r0 + n_rows), weight, 0.0)

    at(3.4, weights)

    def logits(h, first, last):
        r0, n_rows, _ = HALVES[h]

        def one(i, carry):
            k = pl.ds(pl.multiple_of(i * 2048, 2048), 2048)
            n = n_all[:, r0 : r0 + n_rows, k].reshape(NX * n_rows, 2048)
            part = jnp.dot(n, w_all[k, :], preferred_element_type=F32)
            logit[:, r0 : r0 + n_rows, :] += part.reshape(NX, n_rows, 2 * VW)
            return carry

        lax.fori_loop(first, last, one, 0)

    def clear():
        logit[...] = jnp.zeros_like(logit)
        cps["w"].wait_recv()

    entry = lax.broadcasted_iota(jnp.int32, (CAP, 2 * VW), 1)
    base = (x * 2 * NZ * NY + v) * VW
    entry = jnp.where(entry < VW, entry + base, entry + (base + (NZ * NY - 1) * VW)).astype(F32)

    def column(ref, rel, r0, n):
        return to_col(ref[pl.ds(lax.rem(x + rel, NX), 1), :])[r0 : r0 + n]

    def local_stats(h):
        r0, n, _ = HALVES[h]
        stats = [jnp.zeros((8, 128), F32)] * 4
        for rel in range(NX):
            l = logit[rel, r0 : r0 + n, :]
            hit = entry[:n] == column(ids.at[1], rel, r0, n)
            m = jnp.max(l, axis=1, keepdims=True)
            e = jnp.exp(l - m)
            values = (
                m,
                jnp.sum(e, axis=1, keepdims=True),
                jnp.sum(e * l, axis=1, keepdims=True),
                jnp.sum(jnp.where(hit, l, 0.0), axis=1, keepdims=True),
            )
            here = sub8 == lax.rem(x + rel, NX)
            for i in range(4):
                row = jnp.broadcast_to(to_row(values[i], r0), (8, 128))
                stats[i] = jnp.where(here, row, stats[i])
        for i in range(4):
            s1[h, z, i] = stats[i]
        cps["s1", h] = [send(s1.at[h, z], s1.at[h, z], dev(dz=i)) for i in range(1, NZ)]

    def merge(parts):
        peak = parts[0][0]
        for p in parts[1:]:
            peak = jnp.maximum(peak, p[0])
        f = [jnp.exp(p[0] - peak) for p in parts]
        return (
            peak,
            sum(p[1] * g for p, g in zip(parts, f)),
            sum(p[2] * g for p, g in zip(parts, f)),
            sum(p[3] for p in parts),
        )

    own = x * NY + y

    def stats_z(h):
        for cp in cps["s1", h]:
            cp.wait_recv()
        stats = merge([[s1[h, q, i] for i in range(4)] for q in range(NZ)])
        for i in range(4):
            s2[h, own, i] = stats[i]
        cps["s2", h] = [
            send(s2.at[h, own], s2.at[h, own], dev(dx=i, dy=j))
            for i in range(NX) for j in range(NY) if i or j
        ]

    losses = []

    def stats_xy(h):
        for cp in cps["s2", h]:
            cp.wait_recv()
        peak, total, mean, chosen = merge([[s2[h, q, i] for i in range(4)] for q in range(NX * NY)])
        lse = peak + jnp.log(total)
        weight = st[h, 1]
        live = weight != 0.0
        st[h, 0] = lse
        st[h, 2] = jnp.where(live, weight * (mean / total - chosen), 0.0)
        losses.append(jnp.where(live, weight * (lse - chosen), 0.0))
        if h == 1:
            own_loss = losses[0] + losses[1]
            own_loss = jnp.sum(jnp.sum(own_loss, axis=1, keepdims=True), axis=0, keepdims=True)
            loss_x[0] = jnp.broadcast_to(own_loss, (8, 128))
            cps["loss"] = send(loss_x.at[0], loss_x.at[1], dev(dc=1))
        r0, n, _ = HALVES[h]
        for rel in range(NX):
            lse_c, w_c = column(st.at[h, 0], rel, r0, n), column(st.at[h, 1], rel, r0, n)
            hit = jnp.where(entry[:n] == column(ids.at[1], rel, r0, n), 1.0, 0.0)
            p = jnp.exp(logit[rel, r0 : r0 + n, :] - lse_c)
            dl[rel, r0 : r0 + n, :] = (w_c * (p - hit)).astype(BF16)

    def grad_block(h, k, *then):
        r0, n, _ = HALVES[h]
        zz = lax.rem(z + ZORD[k], NZ)
        rows = dl[:, r0 : r0 + n, :].reshape(NX * n, 2 * VW)
        f = pl.ds(pl.multiple_of(zz * NY * VW, NY * VW), NY * VW)
        out = lax.dot_general(rows, w_all[f, :], NT, preferred_element_type=F32).astype(BF16)
        for yy in range(NY):
            ry = lax.rem(yy - y + NY, NY)
            for rx in range(NX):
                block = out[rx * n : (rx + 1) * n, yy * VW : (yy + 1) * VW]
                cut = [block[p[0] - r0 : p[0] - r0 + 16, p[1] : p[1] + p[2]] for p in PARTS[h]]
                b[f"px{h}"][rx, k, ry] = cut[0]
                b[f"pz{h}"][k, rx, ry] = cut[1]
                b[f"py{h}"][ry, rx, k] = cut[2]
        for fn in then:
            fn()

    def add_into(dst, srcs):
        def one(i, carry):
            acc = dst[i].astype(F32)
            for r in srcs:
                acc = acc + r[i].astype(F32)
            dst[i] = acc.astype(BF16)
            return carry

        lax.fori_loop(0, dst.shape[0], one, 0)

    def ring(tag, h, n, axis, block, one_way, buf_a, buf_b, times, done):
        half = n // 2
        side = {1: 0, -1: 1}
        left = [2]

        def begin(sign):
            for i in range(2):
                src = one_way(block(half, i), sign)
                cps[tag, h, sign, 1, i] = send(src, buf_a.at[side[sign], i], dev(**{axis: sign}))

        def arrive(sign, k, i):
            cps[tag, h, sign, k, i].wait_recv()
            d = (sign * (half - k)) % n
            if k == 1:
                add_into(one_way(block(d, i), sign), [buf_a.at[side[sign], i]])
            else:
                add_into(block(d, i), [buf_b.at[side[sign], i, k - 2]])
            cps[tag, h, sign, k + 1, i] = send(
                block(d, i), buf_b.at[side[sign], i, k - 1], dev(**{axis: sign})
            )

        def finish(i):
            for sign in (1, -1):
                cps[tag, h, sign, half, i].wait_recv()
            add_into(block(0, i), [buf_b.at[side[sign], i, half - 2] for sign in (1, -1)])
            left[0] -= 1
            if left[0] == 0:
                done()

        for k in range(1, half):
            for i in range(2):
                for sign in (1, -1):
                    at(times[k - 1] + i * times[-1], arrive, sign, k, i)
        for i in range(2):
            at(times[half - 1] + i * times[-1], finish, i)
        return begin

    def direct(tag, h, n, axis, block, buf, time, done):
        def begin():
            for d in range(1, n):
                cps[tag, h, d] = send(block(d), buf.at[d - 1], dev(**{axis: d}))

        def finish():
            for d in range(1, n):
                cps[tag, h, d].wait_recv()
            acc = block(0)[...].astype(F32)
            for d in range(1, n):
                acc = acc + buf[d - 1].astype(F32)
            done(acc)

        at(time, finish)
        return begin

    def reduce(h, t):
        px, pz, py = b[f"px{h}"], b[f"pz{h}"], b[f"py{h}"]

        def put(i):
            r, l, w = PARTS[h][i]
            def fn(acc):
                dn[r : r + 16, l : l + w] = acc
            return fn

        def back(ref, begin):
            def fn(acc):
                ref[...] = acc.astype(BF16)
                begin()
            return fn

        def cut(m):
            return lambda r, sign: r.at[0:m] if sign == 1 else r.at[m : 2 * m]

        x3 = direct("x3", h, NZ, "dz", lambda d: px.at[0, ZPOS[d], 0], b[f"ex{h}"], t["x3"], put(0))
        x2 = direct("x2", h, NY, "dy", lambda d: px.at[0, :, d], b[f"cx{h}"], t["x2"],
                    back(px.at[0, :, 0], x3))
        x1 = ring("x1", h, NX, "dx", lambda d, i: px.at[d, :, 2 * i : 2 * i + 2], cut(4),
                  b[f"ax{h}"], b[f"bx{h}"], t["x1"], x2)
        z3 = direct("z3", h, NY, "dy", lambda d: pz.at[7, 0, d], b[f"ez{h}"], t["z3"], put(1))
        z2 = direct("z2", h, NX, "dx", lambda d: pz.at[7, d], b[f"cz{h}"], t["z2"],
                    back(pz.at[7, 0], z3))
        z1 = ring("z1", h, NZ, "dz", lambda d, i: pz.at[ZPOS[d], :, 2 * i : 2 * i + 2], cut(2),
                  b[f"az{h}"], b[f"bz{h}"], t["z1"], z2)
        y3 = direct("y3", h, NZ, "dz", lambda d: py.at[0, 0, ZPOS[d]], b[f"ey{h}"], t["y3"], put(2))
        y2 = direct("y2", h, NX, "dx", lambda d: py.at[0, d], b[f"cy{h}"], t["y2"],
                    back(py.at[0, 0], y3))
        y1 = ring("y1", h, NY, "dy", lambda d, i: py.at[d, :, 4 * i : 4 * i + 4], cut(2),
                  b[f"ay{h}"], b[f"by{h}"], t["y1"], y2)
        then = {
            0: (lambda: z1(1), lambda: z1(-1)),
            3: (lambda: x1(1),),
            7: (lambda: x1(-1), lambda: y1(1), lambda: y1(-1)),
        }
        for k in range(NZ):
            at(t["g"] + t["gstep"] * k, grad_block, h, k, *then.get(k, ()))

    def head_chunk(j):
        f = pl.ds(j * 1024, 1024)
        n = n_all[:, :, f].reshape(ROWS, 1024)
        both = lax.dot_general(n, dl[...].reshape(ROWS, 2 * VW), TN, preferred_element_type=F32)
        first, second = both[:, :VW], both[:, VW:]
        mine[f, :] = jnp.where(c == 0, first, second)
        gs[f, :] = jnp.where(c == 0, second, first).astype(BF16)
        cps["g", j] = send(gs.at[f], gr.at[f], dev(dc=1))

    def head_sum(j):
        cps["g", j].wait_recv()

        def one(i, carry):
            f = pl.ds(pl.multiple_of(j * 1024 + i * 256, 256), 256)
            gr[f, :] = (mine[f, :] + gr[f, :].astype(F32)).astype(BF16)
            return carry

        lax.fori_loop(0, 4, one, 0)
        f = pl.ds(j * 1024, 1024)
        cp = pltpu.make_async_copy(gr.at[f], gw_out.at[f], lsem.at[3 + j])
        cp.start()
        outs.append(cp)

    at(12.0, clear)
    at(here0, logits, 0, 0, 4)
    at(here0, local_stats, 0)
    at(here1, logits, 1, 0, 4)
    at(here1, local_stats, 1)
    at(24.0, stats_z, 0)
    at(28.0, stats_z, 1)
    at(30.5, stats_xy, 0)
    at(34.4, stats_xy, 1)
    reduce(0, dict(
        g=31.0, gstep=0.5, z1=(34.5, 38.5, 42.5, 46.5, 0.8), x1=(38.7, 44.5, 1.5), y1=(38.8, 44.6, 1.5),
        x2=50.0, z2=50.1, y2=50.2, x3=55.0, z3=55.1, y3=55.2,
    ))
    reduce(1, dict(
        g=36.0, gstep=0.8, z1=(40.0, 44.0, 48.0, 52.0, 0.8), x1=(45.5, 52.5, 1.5), y1=(45.6, 51.6, 1.0),
        x2=57.0, z2=57.1, y2=56.0, x3=62.0, z3=62.1, y3=61.0,
    ))
    for j in range(8):
        at(42.0 + j * 1.2, head_chunk, j)
        at(53.0 + j * 0.5, head_sum, j)
    run()

    f = pl.ds(pl.multiple_of(v * VW, VW), VW)
    inner = to_col(st[0, 2, pl.ds(x, 1), :] + st[1, 2, pl.ds(x, 1), :])
    unit = hid[:, f].astype(F32) * rinv
    scaled = gain_rows(f, own_exit) * dn[...]
    gh_out[...] = (rinv * (scaled - unit * (inner / D))).astype(BF16)

    cps["loss"].wait_recv()
    loss_out[...] = (loss_x[0] + loss_x[1]) / 512.0
    for cp in outs:
        cp.wait()
    for cp in started:
        cp.wait_send()


def handover(loss, grad_weight, grad_hidden, loss_out, gw_out, gh_out, buf, sem):
    n = D // 4
    parts = [pl.ds(i * n, n) for i in range(4)]
    reads = [pltpu.make_async_copy(grad_weight.at[p], buf.at[p], sem.at[i]) for i, p in enumerate(parts)]
    writes = [pltpu.make_async_copy(buf.at[p], gw_out.at[p], sem.at[4 + i]) for i, p in enumerate(parts)]
    for r in reads:
        r.start()
    gh_out[...] = grad_hidden[...]
    loss_out[...] = loss[0:1, 0:1]
    for r, w in zip(reads, writes):
        r.wait()
        w.start()
    for w in writes:
        w.wait()


def body(hidden, gain, exit_scale, head_weight, targets, exit_ids, counts):
    vmem = pl.BlockSpec(memory_space=pltpu.VMEM)
    smem = pl.BlockSpec(memory_space=pltpu.SMEM)
    hbm = pl.BlockSpec(memory_space=pl.ANY)
    dma = pltpu.SemaphoreType.DMA
    big = jax.ShapeDtypeStruct((D, VW), BF16)
    small = jax.ShapeDtypeStruct((CAP, VW), BF16)
    results = pl.pallas_call(
        kernel,
        out_shape=(jax.ShapeDtypeStruct((8, 128), F32), big, small),
        in_specs=[hbm, hbm, hbm, smem, smem, smem, smem],
        out_specs=(vmem, hbm, vmem),
        scratch_shapes=[pltpu.VMEM(*v) for v in SCRATCH.values()] + [dma((N_SEM,)), dma((N_SEM,)), dma((11,))],
        compiler_params=pltpu.CompilerParams(
            collective_id=0, has_side_effects=True, vmem_limit_bytes=60 * 2**20
        ),
        name="exit_head",
    )(hidden, gain, head_weight, targets, exit_ids, counts, exit_scale)
    loss, grad_weight, grad_hidden = pl.pallas_call(
        handover,
        out_shape=(jax.ShapeDtypeStruct((1, 1), F32), big, small),
        in_specs=[vmem, hbm, vmem],
        out_specs=(vmem, hbm, vmem),
        scratch_shapes=[pltpu.VMEM((D, VW), BF16), dma((8,))],
        compiler_params=pltpu.CompilerParams(vmem_limit_bytes=16 * 2**20),
        name="handover",
    )(*results)
    return (loss.reshape(()), grad_weight, grad_hidden)


def solution(mesh):
    in_specs = (P("section", None), P(), P(), P(None, ("section", "vocab")), P(), P(), P())
    out_specs = (P(), P(None, ("section", "vocab")), P("section", "vocab"))
    return jax.shard_map(body, mesh=mesh, in_specs=in_specs, out_specs=out_specs, check_vma=False)
```

time: 625 us -> 107 us (0.17)
  waiting for transfers between devices: 336 us -> 0 us
  blocking collectives: 226 us -> 0 us
  Pallas kernels: 0 us -> 102 us
  matrix products: 37.3 us -> 0 us
  between operations: 15.7 us -> 0.65 us
  other arithmetic: 7.2 us -> 0 us
    reduce_scatter x2 -> x0, waiting for transfers between devices: 273 us -> none  [the longest x1 253 us: body(): lax.psum_scatter(lax.dot_general(head_weight, dlogits, (((1,), (1,)), (()...]
    psum x2 -> x0, blocking collectives: 149 us -> none  [the longest x1 75.1 us: body(): inner = lax.psum(jnp.sum(scaled * unit, axis=1), 'vocab') / width]
    pallas_call x0 -> x2, Pallas kernels: none -> 102 us  [the longest x1 99.2 us: body(): pl.pallas_call(kernel, out_shape=(jax.ShapeDtypeStruct((8, 128), F32), bi...]
    pmax x1 -> x0, blocking collectives: 76.7 us -> none  [body(): peak = lax.pmax(jnp.max(logits, axis=1), ('section', 'vocab'))]
    all_gather x1 -> x0, waiting for transfers between devices: 63.2 us -> none  [body(): gathered = lax.all_gather(normed, 'section', axis=0, tiled=True)]
    dot_general x4 -> x0, matrix products: 37.3 us -> none  [the longest x1 12.1 us: body(): lax.dot_general(head_weight, dlogits, (((1,), (1,)), ((), ())), preferred...]
  transfers between devices with their start and end apart: 3 -> 0, of which waited for: 3 -> 0; matrix products, arithmetic and copies ran while one was open for 2% -> 0% of each run, Pallas kernels for 0% -> 0%
where the time goes in v2:
time: 107 us; the launch traced here: 106 us
  Pallas kernels  102 us (95%)
  local copies, waits for them, and re-layouts  3.63 us (3%)
    pallas_call x1, Pallas kernels, body(): pl.pallas_call(kernel, out_shape=(jax.ShapeDtypeStruct((8, 128), F32), bi...  99.2 us
    unnamed x6, local copies, waits for them, and re-layouts  3.63 us
    pallas_call x1, Pallas kernels, body(): pl.pallas_call(handover, out_shape=(jax.ShapeDtypeStruct((1, 1), F32), bi...  2.98 us

profile of v2, /device:TPU:2, one launch (start us, length us, event | category | flops | bytes accessed | tf_op | source)
XLA Modules:
  0.0 106.5 jit_solution(11114801192416211298)
XLA Ops:
  0.6 99.2 %exit_head.1 = (f32[8,128]{1,0:T(8,128)}, bf16[8192,256]{1,0:T(8,128)(2,1)}, bf16[80,256]{1,0:T(8,128)(2,1)}) custom-call(bf16[80,8192]{1,0:T(8,128)(2,1)} %hidden.1, f32[4,8192]{1,0:T(4,128)} %gain_in.1, bf16[8192,256]{1,0:T(8,128)(2,1)} %head.1, s32[640]{0:T(1024)} %targets.1, s32[640]{0:T(1024)} %exit_ids.1, s32[8]{0:T(128)} %counts.1, f32[4]{0:T(128)} %scale.1), custom_call_target="tpu_custom_call" | custom-call | tf_op jit(solution)/shard_map/exit_head/pallas_call | solution.py:568
  99.8 0.0 copy-start
  99.9 2.2 %copy-done = bf16[8192,256]{1,0:T(8,128)(2,1)S(1)} copy-done((bf16[8192,256]{1,0:T(8,128)(2,1)S(1)}, bf16[8192,256]{1,0:T(8,128)(2,1)}, u32[]{:S(2)}) %copy-start) | copy-done | bytes 4194328
  102.0 0.0 copy-start.1
  102.0 0.8 copy-done.1
  102.8 0.0 copy-start.2
  102.8 0.7 copy-done.2
  103.5 3.0 %handover.1 = (f32[1,1]{1,0:T(1,128)}, bf16[8192,256]{1,0:T(8,128)(2,1)}, bf16[80,256]{1,0:T(8,128)(2,1)}) custom-call(f32[8,128]{1,0:T(8,128)S(1)} %copy-done.2, bf16[8192,256]{1,0:T(8,128)(2,1)S(1)} %copy-done, bf16[80,256]{1,0:T(8,128)(2,1)S(1)} %copy-done.1), custom_call_target="tpu_custom_call" | custom-call | tf_op jit(solution)/shard_map/handover/pallas_call | solution.py:579
Async XLA Ops:
  99.8 2.2 %copy-start = (bf16[8192,256]{1,0:T(8,128)(2,1)S(1)}, bf16[8192,256]{1,0:T(8,128)(2,1)}, u32[]{:S(2)}) copy-start(bf16[8192,256]{1,0:T(8,128)(2,1)} %get-tuple-element.10.grad_weight) | copy-start | bytes 12582916
  102.0 0.8 copy-start.1
  102.8 0.7 copy-start.2

commit v3 on v2

--- a/solution.py
+++ b/solution.py
@@ -14,24 +14,25 @@
 EXITS = 4
 F32 = jnp.float32
 BF16 = jnp.bfloat16
-ZW, YW = 384, 768
+ZW, YW = 384, 896
 XB0 = NZ * ZW + NY * YW
-XBW = 512
+XBW = 768
+SHIFT = 0
 XA0 = XB0 + XBW
 ZORD = (4, 3, 5, 2, 6, 1, 7, 0)
 ZPOS = {d: k for k, d in enumerate(ZORD)}
-N_SEM = 320
+N_SEND = 40
+N_RECV = 174
 HALVES = ((0, 48, 32), (48, 32, 16))
 PARTS = (((0, 0, 256), (16, 0, 256), (32, 0, 256)), ((48, 0, 256), (64, 0, 128), (64, 128, 128)))
-NT = (((1,), (1,)), ((), ()))
 TN = (((0,), (0,)), ((), ()))
 
 
 def scratch():
     out = dict(
-        hid=((CAP, D), BF16), gain=((EXITS, D), F32), n_all=((NX, CAP, D), BF16), w_all=((D, 2 * VW), BF16),
+        hid=((CAP, D), BF16), gain=((EXITS, D), F32), n_all=((NX, CAP, D), BF16), w_all=((D, 2 * VW), BF16), w_t=((2 * VW, D), BF16),
         logit=((NX, CAP, 2 * VW), F32), dl=((NX, CAP, 2 * VW), BF16),
-        s1=((2, NZ, 4, 8, 128), F32), s2=((2, NX * NY, 4, 8, 128), F32),
+        s1=((2, NZ, 2, 8, 128), F32), s2=((2, NX * NY, 2, 8, 128), F32),
         st=((2, 3, 8, 128), F32), ids=((2, 8, 128), F32), loss=((2, 8, 128), F32), dn=((CAP, VW), F32),
         mine=((D, VW), F32), gs=((D, VW), BF16), gr=((D, VW), BF16),
     )
@@ -61,7 +62,7 @@
 def kernel(hidden, gain_in, head, targets, exit_ids, counts, scale, loss_out, gw_out, gh_out, *refs):
     b = dict(zip(SCRATCH, refs))
     ssem, rsem, lsem = refs[len(SCRATCH) :]
-    hid, gain, n_all, w_all = b["hid"], b["gain"], b["n_all"], b["w_all"]
+    hid, gain, n_all, w_all, w_t = b["hid"], b["gain"], b["n_all"], b["w_all"], b["w_t"]
     logit, dl, s1, s2, st, ids = b["logit"], b["dl"], b["s1"], b["s2"], b["st"], b["ids"]
     dn, mine, gs, gr, loss_x = b["dn"], b["mine"], b["gs"], b["gr"], b["loss"]
     s = lax.axis_index("section")
@@ -75,22 +76,36 @@
             lax.rem(z + dz + NZ, NZ) * NY + lax.rem(y + dy + NY, NY),
         )
 
-    used = [0]
-    started = []
+    slots = [0]
+    pool = [None] * N_SEND
+    count = [0]
+    pending = {}
     outs = []
     cps = {}
     events = []
 
-    def send(src, dst, device):
-        i = used[0]
-        used[0] += 1
+    def slot():
+        slots[0] += 1
+        return slots[0] - 1
+
+    def send(src, dst, device, at_slot=None):
+        at_slot = slot() if at_slot is None else at_slot
+        i = count[0] % N_SEND
+        count[0] += 1
+        if pool[i] is not None:
+            pool[i].wait_send()
         cp = pltpu.make_async_remote_copy(
-            src_ref=src, dst_ref=dst, send_sem=ssem.at[i], recv_sem=rsem.at[i],
+            src_ref=src, dst_ref=dst, send_sem=ssem.at[i], recv_sem=rsem.at[at_slot],
             device_id=device, device_id_type=MESH,
         )
         cp.start()
-        started.append(cp)
-        return cp
+        pool[i] = cp
+        pending.setdefault(at_slot, []).append(cp)
+        return at_slot
+
+    def arrived(at_slot, ref):
+        pltpu.make_async_copy(ref, ref, rsem.at[at_slot]).wait()
+        del pending[at_slot]
 
     def at(time, fn, *args):
         events.append((time, len(events), lambda: fn(*args)))
@@ -121,6 +136,7 @@
     lane = lax.broadcasted_iota(jnp.int32, (8, 128), 1)
     sub8 = lax.broadcasted_iota(jnp.int32, (8, 128), 0)
     flat = sub8 * 128 + lane
+    upper = sub8 < 4
 
     def to_col(row):
         return jnp.sum(jnp.where(diag, jnp.broadcast_to(row, (CAP, 128)), 0.0), axis=1, keepdims=True)
@@ -174,19 +190,25 @@
         return pl.ds(pl.multiple_of(lax.rem(z + d + NZ, NZ) * ZW, ZW), ZW)
 
     def yc(d):
-        return pl.ds(pl.multiple_of(NZ * ZW + lax.rem(y + d + NY, NY) * YW, YW), YW)
+        return pl.ds(pl.multiple_of(NZ * ZW + lax.rem(y + d + NY, NY) * YW, 128), YW)
 
     xb, xa = pl.ds(XB0, XBW), pl.ds(XA0, D - XA0)
 
-    def own_x(tag, h, cols):
+    def own_x(tag, h, cols, far):
         rows = pl.ds(*HALVES[h][:2])
-        cps[tag, h, 1] = send(n_all.at[0, rows, cols], n_all.at[3, rows, cols], dev(dx=1))
-        cps[tag, h, -1] = send(n_all.at[0, rows, cols], n_all.at[1, rows, cols], dev(dx=-1))
+        src = n_all.at[0, rows, cols]
+        k = slot()
+        send(src, n_all.at[3, rows, cols], dev(dx=1), k)
+        send(src, n_all.at[1, rows, cols], dev(dx=-1), k)
+        if far:
+            send(src, n_all.at[2, rows, cols], dev(dx=2), k)
+        cps[tag, h] = k, n_all.at[0 : 3 if far else 2, rows, cols]
 
     def forward_x(tag, h, cols, right):
         rows = pl.ds(*HALVES[h][:2])
         rel, dx = (3, 1) if right else (1, -1)
-        cps[tag, h, 2] = send(n_all.at[rel, rows, cols], n_all.at[2, rows, cols], dev(dx=dx))
+        dst = n_all.at[2, rows, cols]
+        cps[tag, h, 2] = send(n_all.at[rel, rows, cols], dst, dev(dx=dx)), dst
 
     def chain(tag, h, n, cols, axis, rel, t0, step):
         half = n // 2
@@ -196,61 +218,55 @@
         def begin():
             for sign in (1, -1):
                 ref = n_all.at[rel, full, cols(0)]
-                cps[tag, h, rel, sign, 1] = send(ref, ref, dev(**{axis: sign}))
+                cps[tag, h, rel, sign, 1] = send(ref, ref, dev(**{axis: sign})), ref
 
         def arrive(sign, k):
-            cps[tag, h, rel, sign, k].wait_recv()
+            arrived(*cps[tag, h, rel, sign, k])
             if k < half:
                 rows = full if k < half - 1 else (low if sign == 1 else high)
                 ref = n_all.at[rel, rows, cols(-sign * k)]
-                cps[tag, h, rel, sign, k + 1] = send(ref, ref, dev(**{axis: sign}))
+                cps[tag, h, rel, sign, k + 1] = send(ref, ref, dev(**{axis: sign})), ref
 
         for k in range(1, half + 1):
             for sign in (1, -1):
                 at(t0 + step * k, arrive, sign, k)
         return begin
 
-    def gather(h, tz, ty, tb, ta, dz, dy, fwd, zstep, ystep, more):
-        z1 = chain("cz", h, NZ, zc, "dz", 1, tz, zstep)
-        z3 = chain("cz", h, NZ, zc, "dz", 3, tz + 0.1, zstep)
-        z2 = chain("cz", h, NZ, zc, "dz", 2, tz + dz, zstep)
-        y1 = chain("cy", h, NY, yc, "dy", 1, ty, ystep)
-        y3 = chain("cy", h, NY, yc, "dy", 3, ty + 0.1, ystep)
-        y2 = chain("cy", h, NY, yc, "dy", 2, ty + dy, ystep)
-
-        def got(tag, sign, *then):
-            cps[tag, h, sign].wait_recv()
+    def gather(h, tz, ty, tb, ta, fwd, zstep, ystep, after_z, after_y):
+        chains = {}
+        for rel in (1, 3, 2):
+            chains["z", rel] = chain("cz", h, NZ, zc, "dz", rel, tz + 0.1 * rel, zstep)
+            chains["y", rel] = chain("cy", h, NY, yc, "dy", rel, ty + 0.1 * rel, ystep)
+
+        def got(key, *then):
+            arrived(*cps[key])
             for fn in then:
                 fn()
 
-        at(tz, got, "z", -1, z1, lambda: forward_x("z", h, zc(0), False))
-        at(tz, got, "z", 1, z3, *more)
-        at(tz + dz, got, "z", 2, z2)
-        at(ty, got, "y", -1, y1, lambda: forward_x("y", h, yc(0), False))
-        at(ty, got, "y", 1, y3)
-        at(ty + dy, got, "y", 2, y2)
-        at(tb, got, "b", -1, lambda: forward_x("b", h, xb, False))
-        at(tb, got, "b", 1)
-        at(ta, got, "a", 1, lambda: forward_x("a", h, xa, True))
-        at(ta, got, "a", -1)
-        at(tb + fwd, got, "b", 2)
-        at(ta + fwd, got, "a", 2)
+        for tag, t, then in (("z", tz, after_z), ("y", ty, after_y)):
+            at(t, got, (tag, h), chains[tag, 1], chains[tag, 3], chains[tag, 2], then)
+        at(tb, got, ("b", h), lambda: forward_x("b", h, xb, False))
+        at(ta, got, ("a", h), lambda: forward_x("a", h, xa, True))
+        at(tb + fwd, got, ("b", h, 2))
+        at(ta + fwd, got, ("a", h, 2))
         return max(e[0] for e in events) + 0.01
 
     def own_group(h):
-        own_x("b", h, xb)
-        own_x("a", h, xa)
-
-    for h in range(2):
-        own_x("z", h, zc(0))
-        own_x("y", h, yc(0))
-
-    here0 = gather(0, 3.0, 4.5, 7.0, 9.0, 1.6, 2.2, 4.0, 3.0, 4.0, (lambda: own_group(0),))
-    here1 = gather(1, 4.6, 6.5, 12.0, 14.0, 1.6, 2.2, 4.0, 3.6, 4.6, (lambda: own_group(1),))
+        own_x("b", h, xb, False)
+        own_x("a", h, xa, False)
+
+    nop = lambda: None
+    own_x("z", 0, zc(0), True)
+    own_x("y", 0, yc(0), True)
+    own_x("z", 1, zc(0), True)
+    own_x("y", 1, yc(0), True)
+    here0 = SHIFT + gather(0, 4.0, 5.5, 10.0, 10.0, 4.0, 3.0, 4.0, nop, lambda: own_group(0))
+    here1 = SHIFT + gather(1, 6.0, 7.5, 14.0, 14.0, 4.0, 3.2, 4.2, nop, lambda: own_group(1))
 
     def swap_w():
         loads[2].wait()
-        cps["w"] = send(w_all.at[:, own_w], w_all.at[:, own_w], dev(dc=1))
+        mine_w = w_all.at[:, own_w]
+        cps["w"] = send(mine_w, mine_w, dev(dc=1)), mine_w
 
     at(3.2, swap_w)
     at(3.3, spread, 1, targets)
@@ -282,7 +298,11 @@
 
     def clear():
         logit[...] = jnp.zeros_like(logit)
-        cps["w"].wait_recv()
+        arrived(*cps["w"])
+
+    def turn_w(i):
+        f = pl.ds(i * 512, 512)
+        w_t[:, f] = jnp.transpose(w_all[f, :], (1, 0))
 
     entry = lax.broadcasted_iota(jnp.int32, (CAP, 2 * VW), 1)
     base = (x * 2 * NZ * NY + v) * VW
@@ -309,41 +329,40 @@
             for i in range(4):
                 row = jnp.broadcast_to(to_row(values[i], r0), (8, 128))
                 stats[i] = jnp.where(here, row, stats[i])
-        for i in range(4):
-            s1[h, z, i] = stats[i]
-        cps["s1", h] = [send(s1.at[h, z], s1.at[h, z], dev(dz=i)) for i in range(1, NZ)]
-
-    def merge(parts):
-        peak = parts[0][0]
-        for p in parts[1:]:
-            peak = jnp.maximum(peak, p[0])
-        f = [jnp.exp(p[0] - peak) for p in parts]
-        return (
-            peak,
-            sum(p[1] * g for p, g in zip(parts, f)),
-            sum(p[2] * g for p, g in zip(parts, f)),
-            sum(p[3] for p in parts),
-        )
+        s1[h, z, 0] = jnp.where(upper, stats[0], pltpu.roll(stats[1], 4, 0))
+        s1[h, z, 1] = jnp.where(upper, stats[2], pltpu.roll(stats[3], 4, 0))
+        cps["s1", h] = slot()
+        for i in range(1, NZ):
+            send(s1.at[h, z], s1.at[h, z], dev(dz=i), cps["s1", h])
+
+    def merge(ref, n):
+        first = [ref[q, 0] for q in range(n)]
+        peaks = [jnp.where(upper, a, pltpu.roll(a, 4, 0)) for a in first]
+        peak = peaks[0]
+        for p in peaks[1:]:
+            peak = jnp.maximum(peak, p)
+        f = [jnp.exp(p - peak) for p in peaks]
+        total = sum(a * g for a, g in zip(first, f))
+        rest = sum(ref[q, 1] * jnp.where(upper, f[q], 1.0) for q in range(n))
+        return jnp.where(upper, peak, total), rest
 
     own = x * NY + y
 
     def stats_z(h):
-        for cp in cps["s1", h]:
-            cp.wait_recv()
-        stats = merge([[s1[h, q, i] for i in range(4)] for q in range(NZ)])
-        for i in range(4):
-            s2[h, own, i] = stats[i]
-        cps["s2", h] = [
-            send(s2.at[h, own], s2.at[h, own], dev(dx=i, dy=j))
-            for i in range(NX) for j in range(NY) if i or j
-        ]
+        arrived(cps["s1", h], s1.at[h, 0 : NZ - 1])
+        s2[h, own, 0], s2[h, own, 1] = merge(s1.at[h], NZ)
+        cps["s2", h] = slot()
+        for i in range(NX):
+            for j in range(NY):
+                if i or j:
+                    send(s2.at[h, own], s2.at[h, own], dev(dx=i, dy=j), cps["s2", h])
 
     losses = []
 
     def stats_xy(h):
-        for cp in cps["s2", h]:
-            cp.wait_recv()
-        peak, total, mean, chosen = merge([[s2[h, q, i] for i in range(4)] for q in range(NX * NY)])
+        arrived(cps["s2", h], s2.at[h, 0 : NX * NY - 1])
+        peak, mean = merge(s2.at[h], NX * NY)
+        total, chosen = pltpu.roll(peak, 4, 0), pltpu.roll(mean, 4, 0)
         lse = peak + jnp.log(total)
         weight = st[h, 1]
         live = weight != 0.0
@@ -367,7 +386,7 @@
         zz = lax.rem(z + ZORD[k], NZ)
         rows = dl[:, r0 : r0 + n, :].reshape(NX * n, 2 * VW)
         f = pl.ds(pl.multiple_of(zz * NY * VW, NY * VW), NY * VW)
-        out = lax.dot_general(rows, w_all[f, :], NT, preferred_element_type=F32).astype(BF16)
+        out = jnp.dot(rows, w_t[:, f], preferred_element_type=F32).astype(BF16)
         for yy in range(NY):
             ry = lax.rem(yy - y + NY, NY)
             for rx in range(NX):
@@ -400,7 +419,7 @@
                 cps[tag, h, sign, 1, i] = send(src, buf_a.at[side[sign], i], dev(**{axis: sign}))
 
         def arrive(sign, k, i):
-            cps[tag, h, sign, k, i].wait_recv()
+            arrived(cps[tag, h, sign, k, i], buf_a.at[side[sign], i] if k == 1 else buf_b.at[side[sign], i, k - 2])
             d = (sign * (half - k)) % n
             if k == 1:
                 add_into(one_way(block(d, i), sign), [buf_a.at[side[sign], i]])
@@ -412,7 +431,7 @@
 
         def finish(i):
             for sign in (1, -1):
-                cps[tag, h, sign, half, i].wait_recv()
+                arrived(cps[tag, h, sign, half, i], buf_b.at[side[sign], i, half - 2])
             add_into(block(0, i), [buf_b.at[side[sign], i, half - 2] for sign in (1, -1)])
             left[0] -= 1
             if left[0] == 0:
@@ -428,12 +447,12 @@
 
     def direct(tag, h, n, axis, block, buf, time, done):
         def begin():
+            cps[tag, h] = slot()
             for d in range(1, n):
-                cps[tag, h, d] = send(block(d), buf.at[d - 1], dev(**{axis: d}))
+                send(block(d), buf.at[d - 1], dev(**{axis: d}), cps[tag, h])
 
         def finish():
-            for d in range(1, n):
-                cps[tag, h, d].wait_recv()
+            arrived(cps[tag, h], buf)
             acc = block(0)[...].astype(F32)
             for d in range(1, n):
                 acc = acc + buf[d - 1].astype(F32)
@@ -493,7 +512,7 @@
         cps["g", j] = send(gs.at[f], gr.at[f], dev(dc=1))
 
     def head_sum(j):
-        cps["g", j].wait_recv()
+        arrived(cps["g", j], gr.at[pl.ds(j * 1024, 1024)])
 
         def one(i, carry):
             f = pl.ds(pl.multiple_of(j * 1024 + i * 256, 256), 256)
@@ -506,7 +525,9 @@
         cp.start()
         outs.append(cp)
 
-    at(12.0, clear)
+    at(7.6, clear)
+    for i in range(16):
+        at(8.6 + i * 0.5, turn_w, i)
     at(here0, logits, 0, 0, 4)
     at(here0, local_stats, 0)
     at(here1, logits, 1, 0, 4)
@@ -534,26 +555,32 @@
     scaled = gain_rows(f, own_exit) * dn[...]
     gh_out[...] = (rinv * (scaled - unit * (inner / D))).astype(BF16)
 
-    cps["loss"].wait_recv()
+    arrived(cps["loss"], loss_x.at[1])
     loss_out[...] = (loss_x[0] + loss_x[1]) / 512.0
     for cp in outs:
         cp.wait()
-    for cp in started:
-        cp.wait_send()
-
-
-def handover(loss, grad_weight, grad_hidden, loss_out, gw_out, gh_out, buf, sem):
+    for cp in pool:
+        if cp is not None:
+            cp.wait_send()
+    assert not pending and slots[0] <= N_RECV, slots
+
+
+def handover(loss, grad_weight, grad_hidden, loss_out, gw_out, gh_out, buf, small, total, sem):
     n = D // 4
     parts = [pl.ds(i * n, n) for i in range(4)]
     reads = [pltpu.make_async_copy(grad_weight.at[p], buf.at[p], sem.at[i]) for i, p in enumerate(parts)]
     writes = [pltpu.make_async_copy(buf.at[p], gw_out.at[p], sem.at[4 + i]) for i, p in enumerate(parts)]
+    reads += [pltpu.make_async_copy(grad_hidden, small, sem.at[8])]
+    writes += [pltpu.make_async_copy(small, gh_out, sem.at[9])]
+    get_loss = pltpu.make_async_copy(loss, total, sem.at[10])
     for r in reads:
         r.start()
-    gh_out[...] = grad_hidden[...]
-    loss_out[...] = loss[0:1, 0:1]
+    get_loss.start()
     for r, w in zip(reads, writes):
         r.wait()
         w.start()
+    get_loss.wait()
+    loss_out[...] = total[0:1, 0:1]
     for w in writes:
         w.wait()
 
@@ -570,7 +597,7 @@
         out_shape=(jax.ShapeDtypeStruct((8, 128), F32), big, small),
         in_specs=[hbm, hbm, hbm, smem, smem, smem, smem],
         out_specs=(vmem, hbm, vmem),
-        scratch_shapes=[pltpu.VMEM(*v) for v in SCRATCH.values()] + [dma((N_SEM,)), dma((N_SEM,)), dma((11,))],
+        scratch_shapes=[pltpu.VMEM(*v) for v in SCRATCH.values()] + [dma((N_SEND,)), dma((N_RECV,)), dma((11,))],
         compiler_params=pltpu.CompilerParams(
             collective_id=0, has_side_effects=True, vmem_limit_bytes=60 * 2**20
         ),
@@ -579,10 +606,12 @@
     loss, grad_weight, grad_hidden = pl.pallas_call(
         handover,
         out_shape=(jax.ShapeDtypeStruct((1, 1), F32), big, small),
-        in_specs=[vmem, hbm, vmem],
-        out_specs=(vmem, hbm, vmem),
-        scratch_shapes=[pltpu.VMEM((D, VW), BF16), dma((8,))],
-        compiler_params=pltpu.CompilerParams(vmem_limit_bytes=16 * 2**20),
+        in_specs=[hbm, hbm, hbm],
+        out_specs=(vmem, hbm, hbm),
+        scratch_shapes=[
+            pltpu.VMEM((D, VW), BF16), pltpu.VMEM((CAP, VW), BF16), pltpu.VMEM((8, 128), F32), dma((11,)),
+        ],
+        compiler_params=pltpu.CompilerParams(vmem_limit_bytes=58 * 2**20),
         name="handover",
     )(*results)
     return (loss.reshape(()), grad_weight, grad_hidden)

time: 107 us -> 93.5 us (0.87)
  Pallas kernels: 102 us -> 92.6 us
  local copies, waits for them, and re-layouts: 3.63 us -> 0 us
    pallas_call x1, Pallas kernels: 99.2 us -> 88.7 us  [body(): pl.pallas_call(kernel, out_shape=(jax.ShapeDtypeStruct((8, 128), F32), bi...]
    unnamed x6 -> x0, local copies, waits for them, and re-layouts: 3.63 us -> none
where the time goes in v3:
time: 93.5 us; the launch traced here: 93.4 us
  Pallas kernels  92.6 us (99%)
    pallas_call x1, Pallas kernels, body(): pl.pallas_call(kernel, out_shape=(jax.ShapeDtypeStruct((8, 128), F32), bi...  88.7 us
    pallas_call x1, Pallas kernels, body(): pl.pallas_call(handover, out_shape=(jax.ShapeDtypeStruct((1, 1), F32), bi...  3.84 us

profile of v3, /device:TPU:2, one launch (start us, length us, event | category | flops | bytes accessed | tf_op | source)
XLA Modules:
  0.0 93.4 jit_solution(10754327923893539998)
XLA Ops:
  0.6 88.7 %exit_head.1 = (f32[8,128]{1,0:T(8,128)}, bf16[8192,256]{1,0:T(8,128)(2,1)}, bf16[80,256]{1,0:T(8,128)(2,1)}) custom-call(bf16[80,8192]{1,0:T(8,128)(2,1)} %hidden.1, f32[4,8192]{1,0:T(4,128)} %gain_in.1, bf16[8192,256]{1,0:T(8,128)(2,1)} %head.1, s32[640]{0:T(1024)} %targets.1, s32[640]{0:T(1024)} %exit_ids.1, s32[8]{0:T(128)} %counts.1, f32[4]{0:T(128)} %scale.1), custom_call_target="tpu_custom_call" | custom-call | tf_op jit(solution)/shard_map/exit_head/pallas_call | solution.py:595
  89.4 3.8 %handover.1 = (f32[1,1]{1,0:T(1,128)}, bf16[8192,256]{1,0:T(8,128)(2,1)}, bf16[80,256]{1,0:T(8,128)(2,1)}) custom-call(f32[8,128]{1,0:T(8,128)} %get-tuple-element.9.loss, bf16[8192,256]{1,0:T(8,128)(2,1)} %get-tuple-element.10.grad_weight, bf16[80,256]{1,0:T(8,128)(2,1)} %get-tuple-element.11.grad_hidden), custom_call_target="tpu_custom_call" | custom-call | tf_op jit(solution)/shard_map/handover/pallas_call | solution.py:606

commit v4 on v3

--- a/solution.py
+++ b/solution.py
@@ -14,18 +14,61 @@
 EXITS = 4
 F32 = jnp.float32
 BF16 = jnp.bfloat16
-ZW, YW = 384, 896
-XB0 = NZ * ZW + NY * YW
-XBW = 768
-SHIFT = 0
-XA0 = XB0 + XBW
+def widths(zw, yw, bw):
+    return zw, yw, bw, D - NZ * zw - NY * yw - bw
+
+
+WIDTHS = (widths(384, 640, 1280), widths(384, 768, 1152))
 ZORD = (4, 3, 5, 2, 6, 1, 7, 0)
 ZPOS = {d: k for k, d in enumerate(ZORD)}
 N_SEND = 40
 N_RECV = 174
 HALVES = ((0, 48, 32), (48, 32, 16))
-PARTS = (((0, 0, 256), (16, 0, 256), (32, 0, 256)), ((48, 0, 256), (64, 0, 128), (64, 128, 128)))
+PARTS = (((0, 0, 256), (16, 0, 256), (32, 0, 256)), ((48, 0, 128), (64, 0, 256), (48, 128, 128)))
 TN = (((0,), (0,)), ((), ()))
+ORDER = (
+    ("z", 0), ("y", 0), ("cz", 0, 1, 1, 1), ("cz", 0, 1, -1, 1), ("z", 1), ("cz", 0, 3, 1, 1),
+    ("cz", 0, 3, -1, 1), ("w",), ("lg", 0, "z", 0), ("lg", 0, "y", 0), ("cz", 0, 2, 1, 1), ("cz", 0, 2, -1, 1),
+    ("lg", 0, "z", 1), ("lg", 0, "z", 7), ("lg", 1, "z", 0), ("y", 1), ("cz", 0, 1, 1, 2), ("cz", 0, 1, -1, 2),
+    ("lg", 1, "y", 0), ("cy", 0, 1, 1, 1), ("cy", 0, 1, -1, 1), ("cz", 1, 1, 1, 1), ("cz", 1, 1, -1, 1),
+    ("turn", 0), ("turn", 1), ("cz", 1, 3, 1, 1), ("cz", 1, 3, -1, 1), ("cy", 0, 3, 1, 1), ("cy", 0, 3, -1, 1),
+    ("turn", 2), ("cz", 1, 2, 1, 1), ("cz", 1, 2, -1, 1), ("b", 0), ("lg", 1, "z", 1), ("lg", 1, "z", 7),
+    ("cz", 0, 3, 1, 2), ("cz", 0, 3, -1, 2), ("turn", 3), ("cy", 0, 2, 1, 1), ("cy", 0, 2, -1, 1),
+    ("lg", 0, "y", 1), ("cz", 0, 2, 1, 2), ("cz", 0, 2, -1, 2), ("lg", 0, "z", 2), ("cy", 1, 1, 1, 1),
+    ("cy", 1, 1, -1, 1), ("cz", 0, 1, 1, 3), ("cz", 0, 1, -1, 3), ("lg", 0, "z", 6), ("a", 0),
+    ("lg", 0, "y", 3), ("cz", 1, 1, 1, 2), ("cz", 1, 1, -1, 2), ("cy", 1, 3, 1, 1), ("cy", 1, 3, -1, 1),
+    ("turn", 4), ("cz", 1, 3, 1, 2), ("cz", 1, 3, -1, 2), ("turn", 5), ("cz", 1, 2, 1, 2), ("cz", 1, 2, -1, 2),
+    ("lg", 1, "z", 2), ("cy", 1, 2, 1, 1), ("cy", 1, 2, -1, 1), ("b", 1), ("lg", 1, "z", 6),
+    ("cy", 0, 1, -1, 2), ("cz", 0, 3, 1, 3), ("cz", 0, 3, -1, 3), ("lg", 1, "y", 1), ("cy", 0, 1, 1, 2),
+    ("cy", 0, 3, -1, 2), ("cz", 0, 2, 1, 3), ("a", 1), ("cz", 0, 2, -1, 3), ("cy", 0, 2, -1, 2),
+    ("lg", 0, "z", 3), ("cz", 0, 1, -1, 4), ("lg", 0, "z", 5), ("cy", 0, 3, 1, 2), ("cz", 0, 1, 1, 4),
+    ("cy", 1, 1, -1, 2), ("lg", 1, "y", 3), ("cz", 1, 1, -1, 3), ("cz", 1, 1, 1, 3), ("cy", 1, 3, -1, 2),
+    ("turn", 6), ("cz", 1, 3, -1, 3), ("cy", 0, 2, 1, 2), ("cz", 1, 3, 1, 3), ("lg", 0, "y", 2),
+    ("cz", 1, 2, -1, 3), ("cy", 1, 1, 1, 2), ("cy", 1, 2, -1, 2), ("cz", 1, 2, 1, 3), ("cz", 0, 3, -1, 4),
+    ("lg", 1, "z", 3), ("cy", 1, 3, 1, 2), ("a", 0, 2), ("cz", 0, 3, 1, 4), ("b", 0, 2), ("cz", 0, 2, -1, 4),
+    ("lg", 0, "x"), ("cy", 1, 2, 1, 2), ("cz", 0, 2, 1, 4), ("lg", 0, "z", 4), ("ls", 0), ("cz", 1, 1, -1, 4),
+    ("cz", 1, 1, 1, 4), ("a", 1, 2), ("b", 1, 2), ("cz", 1, 3, -1, 4), ("cz", 1, 3, 1, 4), ("cz", 1, 2, -1, 4),
+    ("lg", 1, "z", 5), ("cz", 1, 2, 1, 4), ("lg", 1, "z", 4), ("lg", 1, "y", 2), ("lg", 1, "x"), ("ls", 1),
+    ("turn", 7), ("turn", 8), ("turn", 9), ("turn", 10), ("turn", 11), ("turn", 12), ("turn", 13), ("sz", 0),
+    ("turn", 14), ("turn", 15), ("sz", 1), ("sxy", 0), ("gb", 0, 0), ("gb", 0, 1), ("gb", 0, 2), ("gb", 0, 3),
+    ("gb", 0, 4), ("sxy", 1), ("gb", 0, 5), ("gb", 0, 6), ("z1", 0, 1, 1, 0), ("z1", 0, -1, 1, 0), ("gb", 0, 7),
+    ("gb", 1, 0), ("z1", 0, 1, 1, 1), ("z1", 0, -1, 1, 1), ("gb", 1, 1), ("gb", 1, 2), ("x1", 0, 1, 1, 0),
+    ("gb", 1, 3), ("gb", 1, 4), ("gb", 1, 5), ("gb", 1, 6), ("x1", 0, 1, 1, 1), ("gb", 1, 7), ("head", 0),
+    ("z1", 0, 1, 2, 0), ("z1", 0, -1, 2, 0), ("x1", 0, -1, 1, 0), ("y1", 0, 1, 1, 0), ("y1", 0, -1, 1, 0),
+    ("z1", 1, 1, 1, 0), ("z1", 1, -1, 1, 0), ("z1", 1, 1, 1, 1), ("z1", 1, -1, 1, 1), ("head", 1),
+    ("x1", 0, -1, 1, 1), ("y1", 0, 1, 1, 1), ("y1", 0, -1, 1, 1), ("z1", 0, 1, 2, 1), ("x1", 1, -1, 1, 0),
+    ("z1", 0, -1, 2, 1), ("y1", 1, 1, 1, 0), ("y1", 1, -1, 1, 0), ("head", 2), ("x1", 1, -1, 1, 1),
+    ("y1", 1, 1, 1, 1), ("y1", 1, -1, 1, 1), ("x1", 1, 1, 1, 0), ("z1", 0, 1, 3, 0), ("x1", 1, 1, 1, 1),
+    ("z1", 0, -1, 3, 0), ("head", 3), ("head", 4), ("z1", 1, 1, 2, 0), ("z1", 1, -1, 2, 0), ("x1", 0, "fin", 0),
+    ("y1", 0, "fin", 0), ("z1", 1, 1, 2, 1), ("z1", 1, -1, 2, 1), ("head", 5), ("head", 6), ("z1", 0, 1, 3, 1),
+    ("z1", 0, -1, 3, 1), ("x1", 0, "fin", 1), ("y1", 0, "fin", 1), ("head", 7), ("z1", 0, "fin", 0),
+    ("x1", 1, "fin", 0), ("y1", 1, "fin", 0), ("sum", 0), ("z1", 1, 1, 3, 0), ("z1", 1, -1, 3, 0),
+    ("x1", 1, "fin", 1), ("y1", 1, "fin", 1), ("sum", 1), ("sum", 2), ("z1", 1, 1, 3, 1), ("z1", 1, -1, 3, 1),
+    ("sum", 3), ("sum", 4), ("sum", 5), ("sum", 6), ("sum", 7), ("z1", 0, "fin", 1), ("x2", 0), ("y2", 0),
+    ("z1", 1, "fin", 0), ("x2", 1), ("y2", 1), ("z1", 1, "fin", 1), ("z2", 0), ("x3", 0), ("z2", 1), ("z3", 0),
+    ("y3", 0), ("x3", 1), ("y3", 1), ("z3", 1),
+)
+RANK = {key: i for i, key in enumerate(ORDER)}
 
 
 def scratch():
@@ -48,10 +91,10 @@
         out[f"ay{h}"] = ((2, 2, 2, 4, 16, ly), BF16)
         out[f"by{h}"] = ((2, 2, 1, NX, 4, 16, ly), BF16)
         out[f"cx{h}"] = ((NY - 1, NZ, 16, lx), BF16)
-        out[f"cz{h}"] = ((NX - 1, NY, 16, lz), BF16)
+        out[f"cz{h}"] = ((NY - 1, NX, 16, lz), BF16)
         out[f"cy{h}"] = ((NX - 1, NZ, 16, ly), BF16)
         out[f"ex{h}"] = ((NZ - 1, 16, lx), BF16)
-        out[f"ez{h}"] = ((NY - 1, 16, lz), BF16)
+        out[f"ez{h}"] = ((NX - 1, 16, lz), BF16)
         out[f"ey{h}"] = ((NZ - 1, 16, ly), BF16)
     return out
 
@@ -107,13 +150,13 @@
         pltpu.make_async_copy(ref, ref, rsem.at[at_slot]).wait()
         del pending[at_slot]
 
-    def at(time, fn, *args):
-        events.append((time, len(events), lambda: fn(*args)))
+    def at(key, fn, *args):
+        events.append((RANK[key], lambda: fn(*args)))
 
     def run():
-        for _, _, fn in sorted(events, key=lambda e: (e[0], e[1])):
+        assert len(events) == len(RANK)
+        for t_, fn in sorted(events, key=lambda e: e[0]):
             fn()
-        events.clear()
 
     barrier = pltpu.get_barrier_semaphore()
     friends = [dict(dc=1)]
@@ -186,16 +229,16 @@
     lax.fori_loop(0, D // 512, norm_chunk, 0)
     pl.semaphore_wait(barrier, len(friends))
 
-    def zc(d):
-        return pl.ds(pl.multiple_of(lax.rem(z + d + NZ, NZ) * ZW, ZW), ZW)
-
-    def yc(d):
-        return pl.ds(pl.multiple_of(NZ * ZW + lax.rem(y + d + NY, NY) * YW, 128), YW)
-
-    xb, xa = pl.ds(XB0, XBW), pl.ds(XA0, D - XA0)
-
-    def own_x(tag, h, cols, far):
-        rows = pl.ds(*HALVES[h][:2])
+    def columns(h, tag, d=0):
+        zw, yw, bw, aw = WIDTHS[h]
+        if tag == "z":
+            return pl.ds(pl.multiple_of(lax.rem(z + d + NZ, NZ) * zw, 128), zw)
+        if tag == "y":
+            return pl.ds(pl.multiple_of(NZ * zw + lax.rem(y + d + NY, NY) * yw, 128), yw)
+        return pl.ds(D - aw - bw, bw) if tag == "b" else pl.ds(D - aw, aw)
+
+    def own_x(tag, h):
+        rows, cols, far = pl.ds(*HALVES[h][:2]), columns(h, tag), tag in "zy"
         src = n_all.at[0, rows, cols]
         k = slot()
         send(src, n_all.at[3, rows, cols], dev(dx=1), k)
@@ -204,74 +247,81 @@
             send(src, n_all.at[2, rows, cols], dev(dx=2), k)
         cps[tag, h] = k, n_all.at[0 : 3 if far else 2, rows, cols]
 
-    def forward_x(tag, h, cols, right):
-        rows = pl.ds(*HALVES[h][:2])
-        rel, dx = (3, 1) if right else (1, -1)
-        dst = n_all.at[2, rows, cols]
-        cps[tag, h, 2] = send(n_all.at[rel, rows, cols], dst, dev(dx=dx)), dst
-
-    def chain(tag, h, n, cols, axis, rel, t0, step):
+    def chain(tag, h, n, axis, rel):
         half = n // 2
         r0, n_rows, n_low = HALVES[h]
         full, low, high = pl.ds(r0, n_rows), pl.ds(r0, n_low), pl.ds(r0 + n_low, n_rows - n_low)
 
         def begin():
             for sign in (1, -1):
-                ref = n_all.at[rel, full, cols(0)]
+                ref = n_all.at[rel, full, columns(h, tag)]
                 cps[tag, h, rel, sign, 1] = send(ref, ref, dev(**{axis: sign})), ref
 
         def arrive(sign, k):
             arrived(*cps[tag, h, rel, sign, k])
             if k < half:
                 rows = full if k < half - 1 else (low if sign == 1 else high)
-                ref = n_all.at[rel, rows, cols(-sign * k)]
+                ref = n_all.at[rel, rows, columns(h, tag, -sign * k)]
                 cps[tag, h, rel, sign, k + 1] = send(ref, ref, dev(**{axis: sign})), ref
 
         for k in range(1, half + 1):
             for sign in (1, -1):
-                at(t0 + step * k, arrive, sign, k)
+                at(("c" + tag, h, rel, sign, k), arrive, sign, k)
         return begin
 
-    def gather(h, tz, ty, tb, ta, fwd, zstep, ystep, after_z, after_y):
-        chains = {}
-        for rel in (1, 3, 2):
-            chains["z", rel] = chain("cz", h, NZ, zc, "dz", rel, tz + 0.1 * rel, zstep)
-            chains["y", rel] = chain("cy", h, NY, yc, "dy", rel, ty + 0.1 * rel, ystep)
-
-        def got(key, *then):
-            arrived(*cps[key])
+    def gather(h):
+        def got(tag, then):
+            arrived(*cps[tag, h])
             for fn in then:
                 fn()
 
-        for tag, t, then in (("z", tz, after_z), ("y", ty, after_y)):
-            at(t, got, (tag, h), chains[tag, 1], chains[tag, 3], chains[tag, 2], then)
-        at(tb, got, ("b", h), lambda: forward_x("b", h, xb, False))
-        at(ta, got, ("a", h), lambda: forward_x("a", h, xa, True))
-        at(tb + fwd, got, ("b", h, 2))
-        at(ta + fwd, got, ("a", h, 2))
-        return max(e[0] for e in events) + 0.01
-
-    def own_group(h):
-        own_x("b", h, xb, False)
-        own_x("a", h, xa, False)
-
-    nop = lambda: None
-    own_x("z", 0, zc(0), True)
-    own_x("y", 0, yc(0), True)
-    own_x("z", 1, zc(0), True)
-    own_x("y", 1, yc(0), True)
-    here0 = SHIFT + gather(0, 4.0, 5.5, 10.0, 10.0, 4.0, 3.0, 4.0, nop, lambda: own_group(0))
-    here1 = SHIFT + gather(1, 6.0, 7.5, 14.0, 14.0, 4.0, 3.2, 4.2, nop, lambda: own_group(1))
-
-    def swap_w():
-        loads[2].wait()
-        mine_w = w_all.at[:, own_w]
-        cps["w"] = send(mine_w, mine_w, dev(dc=1)), mine_w
-
-    at(3.2, swap_w)
-    at(3.3, spread, 1, targets)
+        def got_x(tag):
+            arrived(*cps[tag, h])
+            rows, cols = pl.ds(*HALVES[h][:2]), columns(h, tag)
+            rel, dx = (1, -1) if tag == "b" else (3, 1)
+            dst = n_all.at[2, rows, cols]
+            cps[tag, h, 2] = send(n_all.at[rel, rows, cols], dst, dev(dx=dx)), dst
+
+        own_rest = [lambda: own_x("b", h), lambda: own_x("a", h)]
+        for tag, n, axis, more in (("z", NZ, "dz", []), ("y", NY, "dy", own_rest)):
+            at((tag, h), got, tag, [chain(tag, h, n, axis, rel) for rel in (1, 3, 2)] + more)
+            for d in range(n):
+                at(("lg", h, tag, d), logits, h, tag, d)
+        for tag in "ba":
+            at((tag, h), got_x, tag)
+            at((tag, h, 2), lambda tag=tag: arrived(*cps[tag, h, 2]))
+        at(("lg", h, "x"), logits, h, "x", 0)
+
+    def logits(h, tag, d):
+        r0, n_rows, _ = HALVES[h]
+        first = D - sum(WIDTHS[h][2:])
+        k = pl.ds(first, D - first) if tag == "x" else columns(h, tag, d)
+        n = n_all[:, r0 : r0 + n_rows, k].reshape(NX * n_rows, k.size)
+        part = jnp.dot(n, w_all[k, :], preferred_element_type=F32)
+        logit[:, r0 : r0 + n_rows, :] += part.reshape(NX, n_rows, 2 * VW)
+
+    def take_w():
+        arrived(*cps["w"])
+        logit[...] = jnp.zeros_like(logit)
+
+    def turn_w(i):
+        f = pl.ds(i * 512, 512)
+        w_t[:, f] = jnp.transpose(w_all[f, :], (1, 0))
+
+    for h in range(2):
+        own_x("z", h)
+        own_x("y", h)
+    for h in range(2):
+        gather(h)
+    loads[2].wait()
+    mine_w = w_all.at[:, own_w]
+    cps["w"] = send(mine_w, mine_w, dev(dc=1)), mine_w
+    at(("w",), take_w)
+    for i in range(16):
+        at(("turn", i), turn_w, i)
 
     def weights():
+        spread(1, targets)
         weight = jnp.zeros((8, 128), F32)
         exits = ids[0]
         for i in range(EXITS):
@@ -282,27 +332,7 @@
             r0, n_rows, _ = HALVES[h]
             st[h, 1] = jnp.where((sub8 < NX) & (lane >= r0) & (lane < r0 + n_rows), weight, 0.0)
 
-    at(3.4, weights)
-
-    def logits(h, first, last):
-        r0, n_rows, _ = HALVES[h]
-
-        def one(i, carry):
-            k = pl.ds(pl.multiple_of(i * 2048, 2048), 2048)
-            n = n_all[:, r0 : r0 + n_rows, k].reshape(NX * n_rows, 2048)
-            part = jnp.dot(n, w_all[k, :], preferred_element_type=F32)
-            logit[:, r0 : r0 + n_rows, :] += part.reshape(NX, n_rows, 2 * VW)
-            return carry
-
-        lax.fori_loop(first, last, one, 0)
-
-    def clear():
-        logit[...] = jnp.zeros_like(logit)
-        arrived(*cps["w"])
-
-    def turn_w(i):
-        f = pl.ds(i * 512, 512)
-        w_t[:, f] = jnp.transpose(w_all[f, :], (1, 0))
+    weights()
 
     entry = lax.broadcasted_iota(jnp.int32, (CAP, 2 * VW), 1)
     base = (x * 2 * NZ * NY + v) * VW
@@ -408,7 +438,7 @@
 
         lax.fori_loop(0, dst.shape[0], one, 0)
 
-    def ring(tag, h, n, axis, block, one_way, buf_a, buf_b, times, done):
+    def ring(tag, h, n, axis, block, one_way, buf_a, buf_b, done):
         half = n // 2
         side = {1: 0, -1: 1}
         left = [2]
@@ -440,12 +470,12 @@
         for k in range(1, half):
             for i in range(2):
                 for sign in (1, -1):
-                    at(times[k - 1] + i * times[-1], arrive, sign, k, i)
+                    at((tag, h, sign, k, i), arrive, sign, k, i)
         for i in range(2):
-            at(times[half - 1] + i * times[-1], finish, i)
+            at((tag, h, "fin", i), finish, i)
         return begin
 
-    def direct(tag, h, n, axis, block, buf, time, done):
+    def direct(tag, h, n, axis, block, buf, done):
         def begin():
             cps[tag, h] = slot()
             for d in range(1, n):
@@ -458,10 +488,10 @@
                 acc = acc + buf[d - 1].astype(F32)
             done(acc)
 
-        at(time, finish)
+        at((tag, h), finish)
         return begin
 
-    def reduce(h, t):
+    def reduce(h):
         px, pz, py = b[f"px{h}"], b[f"pz{h}"], b[f"py{h}"]
 
         def put(i):
@@ -479,28 +509,25 @@
         def cut(m):
             return lambda r, sign: r.at[0:m] if sign == 1 else r.at[m : 2 * m]
 
-        x3 = direct("x3", h, NZ, "dz", lambda d: px.at[0, ZPOS[d], 0], b[f"ex{h}"], t["x3"], put(0))
-        x2 = direct("x2", h, NY, "dy", lambda d: px.at[0, :, d], b[f"cx{h}"], t["x2"],
-                    back(px.at[0, :, 0], x3))
+        x3 = direct("x3", h, NZ, "dz", lambda d: px.at[0, ZPOS[d], 0], b[f"ex{h}"], put(0))
+        x2 = direct("x2", h, NY, "dy", lambda d: px.at[0, :, d], b[f"cx{h}"], back(px.at[0, :, 0], x3))
         x1 = ring("x1", h, NX, "dx", lambda d, i: px.at[d, :, 2 * i : 2 * i + 2], cut(4),
-                  b[f"ax{h}"], b[f"bx{h}"], t["x1"], x2)
-        z3 = direct("z3", h, NY, "dy", lambda d: pz.at[7, 0, d], b[f"ez{h}"], t["z3"], put(1))
-        z2 = direct("z2", h, NX, "dx", lambda d: pz.at[7, d], b[f"cz{h}"], t["z2"],
-                    back(pz.at[7, 0], z3))
+                  b[f"ax{h}"], b[f"bx{h}"], x2)
+        z3 = direct("z3", h, NX, "dx", lambda d: pz.at[7, d, 0], b[f"ez{h}"], put(1))
+        z2 = direct("z2", h, NY, "dy", lambda d: pz.at[7, :, d], b[f"cz{h}"], back(pz.at[7, :, 0], z3))
         z1 = ring("z1", h, NZ, "dz", lambda d, i: pz.at[ZPOS[d], :, 2 * i : 2 * i + 2], cut(2),
-                  b[f"az{h}"], b[f"bz{h}"], t["z1"], z2)
-        y3 = direct("y3", h, NZ, "dz", lambda d: py.at[0, 0, ZPOS[d]], b[f"ey{h}"], t["y3"], put(2))
-        y2 = direct("y2", h, NX, "dx", lambda d: py.at[0, d], b[f"cy{h}"], t["y2"],
-                    back(py.at[0, 0], y3))
+                  b[f"az{h}"], b[f"bz{h}"], z2)
+        y3 = direct("y3", h, NZ, "dz", lambda d: py.at[0, 0, ZPOS[d]], b[f"ey{h}"], put(2))
+        y2 = direct("y2", h, NX, "dx", lambda d: py.at[0, d], b[f"cy{h}"], back(py.at[0, 0], y3))
         y1 = ring("y1", h, NY, "dy", lambda d, i: py.at[d, :, 4 * i : 4 * i + 4], cut(2),
-                  b[f"ay{h}"], b[f"by{h}"], t["y1"], y2)
+                  b[f"ay{h}"], b[f"by{h}"], y2)
         then = {
             0: (lambda: z1(1), lambda: z1(-1)),
             3: (lambda: x1(1),),
             7: (lambda: x1(-1), lambda: y1(1), lambda: y1(-1)),
         }
         for k in range(NZ):
-            at(t["g"] + t["gstep"] * k, grad_block, h, k, *then.get(k, ()))
+            at(("gb", h, k), grad_block, h, k, *then.get(k, ()))
 
     def head_chunk(j):
         f = pl.ds(j * 1024, 1024)
@@ -525,28 +552,14 @@
         cp.start()
         outs.append(cp)
 
-    at(7.6, clear)
-    for i in range(16):
-        at(8.6 + i * 0.5, turn_w, i)
-    at(here0, logits, 0, 0, 4)
-    at(here0, local_stats, 0)
-    at(here1, logits, 1, 0, 4)
-    at(here1, local_stats, 1)
-    at(24.0, stats_z, 0)
-    at(28.0, stats_z, 1)
-    at(30.5, stats_xy, 0)
-    at(34.4, stats_xy, 1)
-    reduce(0, dict(
-        g=31.0, gstep=0.5, z1=(34.5, 38.5, 42.5, 46.5, 0.8), x1=(38.7, 44.5, 1.5), y1=(38.8, 44.6, 1.5),
-        x2=50.0, z2=50.1, y2=50.2, x3=55.0, z3=55.1, y3=55.2,
-    ))
-    reduce(1, dict(
-        g=36.0, gstep=0.8, z1=(40.0, 44.0, 48.0, 52.0, 0.8), x1=(45.5, 52.5, 1.5), y1=(45.6, 51.6, 1.0),
-        x2=57.0, z2=57.1, y2=56.0, x3=62.0, z3=62.1, y3=61.0,
-    ))
+    for h in range(2):
+        at(("ls", h), local_stats, h)
+        at(("sz", h), stats_z, h)
+        at(("sxy", h), stats_xy, h)
+        reduce(h)
     for j in range(8):
-        at(42.0 + j * 1.2, head_chunk, j)
-        at(53.0 + j * 0.5, head_sum, j)
+        at(("head", j), head_chunk, j)
+        at(("sum", j), head_sum, j)
     run()
 
     f = pl.ds(pl.multiple_of(v * VW, VW), VW)

time: 93.5 us -> 82.5 us (0.88)
  Pallas kernels: 92.6 us -> 80.8 us
    pallas_call x1, Pallas kernels: 88.7 us -> 77 us  [body(): pl.pallas_call(kernel, out_shape=(jax.ShapeDtypeStruct((8, 128), F32), bi...]
where the time goes in v4:
time: 82.5 us; the launch traced here: 81.6 us
  Pallas kernels  80.8 us (98%)
    pallas_call x1, Pallas kernels, body(): pl.pallas_call(kernel, out_shape=(jax.ShapeDtypeStruct((8, 128), F32), bi...  77 us
    pallas_call x1, Pallas kernels, body(): pl.pallas_call(handover, out_shape=(jax.ShapeDtypeStruct((1, 1), F32), bi...  3.84 us

profile of v4, /device:TPU:2, one launch (start us, length us, event | category | flops | bytes accessed | tf_op | source)
XLA Modules:
  0.0 81.6 jit_solution(3969681637526520335)
XLA Ops:
  0.6 77.0 %exit_head.1 = (f32[8,128]{1,0:T(8,128)}, bf16[8192,256]{1,0:T(8,128)(2,1)}, bf16[80,256]{1,0:T(8,128)(2,1)}) custom-call(bf16[80,8192]{1,0:T(8,128)(2,1)} %hidden.1, f32[4,8192]{1,0:T(4,128)} %gain_in.1, bf16[8192,256]{1,0:T(8,128)(2,1)} %head.1, s32[640]{0:T(1024)} %targets.1, s32[640]{0:T(1024)} %exit_ids.1, s32[8]{0:T(128)} %counts.1, f32[4]{0:T(128)} %scale.1), custom_call_target="tpu_custom_call" | custom-call | tf_op jit(solution)/shard_map/exit_head/pallas_call | solution.py:608
  77.6 3.8 %handover.1 = (f32[1,1]{1,0:T(1,128)}, bf16[8192,256]{1,0:T(8,128)(2,1)}, bf16[80,256]{1,0:T(8,128)(2,1)}) custom-call(f32[8,128]{1,0:T(8,128)} %get-tuple-element.9.loss, bf16[8192,256]{1,0:T(8,128)(2,1)} %get-tuple-element.10.grad_weight, bf16[80,256]{1,0:T(8,128)(2,1)} %get-tuple-element.11.grad_hidden), custom_call_target="tpu_custom_call" | custom-call | tf_op jit(solution)/shard_map/handover/pallas_call | solution.py:619

commit v5 on v4

--- a/solution.py
+++ b/solution.py
@@ -18,55 +18,59 @@
     return zw, yw, bw, D - NZ * zw - NY * yw - bw
 
 
-WIDTHS = (widths(384, 640, 1280), widths(384, 768, 1152))
+WIDTHS = (widths(384, 768, 1152), widths(384, 768, 1408))
 ZORD = (4, 3, 5, 2, 6, 1, 7, 0)
 ZPOS = {d: k for k, d in enumerate(ZORD)}
 N_SEND = 40
-N_RECV = 174
+N_RECV = 176
 HALVES = ((0, 48, 32), (48, 32, 16))
 PARTS = (((0, 0, 256), (16, 0, 256), (32, 0, 256)), ((48, 0, 128), (64, 0, 256), (48, 128, 128)))
+FIRST = (('z', 0), ('y', 0), ('z', 1))
+AFTER = {('z', 0): (('b', 0), ('a', 0)), ('y', 0): (('y', 1), ('b', 1), ('a', 1))}
+CHAINS = ((4, 1, 2), (1, 2, 4))
+Z_AT_ONCE = (0, 1)
 TN = (((0,), (0,)), ((), ()))
 ORDER = (
-    ("z", 0), ("y", 0), ("cz", 0, 1, 1, 1), ("cz", 0, 1, -1, 1), ("z", 1), ("cz", 0, 3, 1, 1),
-    ("cz", 0, 3, -1, 1), ("w",), ("lg", 0, "z", 0), ("lg", 0, "y", 0), ("cz", 0, 2, 1, 1), ("cz", 0, 2, -1, 1),
-    ("lg", 0, "z", 1), ("lg", 0, "z", 7), ("lg", 1, "z", 0), ("y", 1), ("cz", 0, 1, 1, 2), ("cz", 0, 1, -1, 2),
-    ("lg", 1, "y", 0), ("cy", 0, 1, 1, 1), ("cy", 0, 1, -1, 1), ("cz", 1, 1, 1, 1), ("cz", 1, 1, -1, 1),
-    ("turn", 0), ("turn", 1), ("cz", 1, 3, 1, 1), ("cz", 1, 3, -1, 1), ("cy", 0, 3, 1, 1), ("cy", 0, 3, -1, 1),
-    ("turn", 2), ("cz", 1, 2, 1, 1), ("cz", 1, 2, -1, 1), ("b", 0), ("lg", 1, "z", 1), ("lg", 1, "z", 7),
-    ("cz", 0, 3, 1, 2), ("cz", 0, 3, -1, 2), ("turn", 3), ("cy", 0, 2, 1, 1), ("cy", 0, 2, -1, 1),
-    ("lg", 0, "y", 1), ("cz", 0, 2, 1, 2), ("cz", 0, 2, -1, 2), ("lg", 0, "z", 2), ("cy", 1, 1, 1, 1),
-    ("cy", 1, 1, -1, 1), ("cz", 0, 1, 1, 3), ("cz", 0, 1, -1, 3), ("lg", 0, "z", 6), ("a", 0),
-    ("lg", 0, "y", 3), ("cz", 1, 1, 1, 2), ("cz", 1, 1, -1, 2), ("cy", 1, 3, 1, 1), ("cy", 1, 3, -1, 1),
-    ("turn", 4), ("cz", 1, 3, 1, 2), ("cz", 1, 3, -1, 2), ("turn", 5), ("cz", 1, 2, 1, 2), ("cz", 1, 2, -1, 2),
-    ("lg", 1, "z", 2), ("cy", 1, 2, 1, 1), ("cy", 1, 2, -1, 1), ("b", 1), ("lg", 1, "z", 6),
-    ("cy", 0, 1, -1, 2), ("cz", 0, 3, 1, 3), ("cz", 0, 3, -1, 3), ("lg", 1, "y", 1), ("cy", 0, 1, 1, 2),
-    ("cy", 0, 3, -1, 2), ("cz", 0, 2, 1, 3), ("a", 1), ("cz", 0, 2, -1, 3), ("cy", 0, 2, -1, 2),
-    ("lg", 0, "z", 3), ("cz", 0, 1, -1, 4), ("lg", 0, "z", 5), ("cy", 0, 3, 1, 2), ("cz", 0, 1, 1, 4),
-    ("cy", 1, 1, -1, 2), ("lg", 1, "y", 3), ("cz", 1, 1, -1, 3), ("cz", 1, 1, 1, 3), ("cy", 1, 3, -1, 2),
-    ("turn", 6), ("cz", 1, 3, -1, 3), ("cy", 0, 2, 1, 2), ("cz", 1, 3, 1, 3), ("lg", 0, "y", 2),
-    ("cz", 1, 2, -1, 3), ("cy", 1, 1, 1, 2), ("cy", 1, 2, -1, 2), ("cz", 1, 2, 1, 3), ("cz", 0, 3, -1, 4),
-    ("lg", 1, "z", 3), ("cy", 1, 3, 1, 2), ("a", 0, 2), ("cz", 0, 3, 1, 4), ("b", 0, 2), ("cz", 0, 2, -1, 4),
-    ("lg", 0, "x"), ("cy", 1, 2, 1, 2), ("cz", 0, 2, 1, 4), ("lg", 0, "z", 4), ("ls", 0), ("cz", 1, 1, -1, 4),
-    ("cz", 1, 1, 1, 4), ("a", 1, 2), ("b", 1, 2), ("cz", 1, 3, -1, 4), ("cz", 1, 3, 1, 4), ("cz", 1, 2, -1, 4),
-    ("lg", 1, "z", 5), ("cz", 1, 2, 1, 4), ("lg", 1, "z", 4), ("lg", 1, "y", 2), ("lg", 1, "x"), ("ls", 1),
-    ("turn", 7), ("turn", 8), ("turn", 9), ("turn", 10), ("turn", 11), ("turn", 12), ("turn", 13), ("sz", 0),
-    ("turn", 14), ("turn", 15), ("sz", 1), ("sxy", 0), ("gb", 0, 0), ("gb", 0, 1), ("gb", 0, 2), ("gb", 0, 3),
-    ("gb", 0, 4), ("sxy", 1), ("gb", 0, 5), ("gb", 0, 6), ("z1", 0, 1, 1, 0), ("z1", 0, -1, 1, 0), ("gb", 0, 7),
-    ("gb", 1, 0), ("z1", 0, 1, 1, 1), ("z1", 0, -1, 1, 1), ("gb", 1, 1), ("gb", 1, 2), ("x1", 0, 1, 1, 0),
-    ("gb", 1, 3), ("gb", 1, 4), ("gb", 1, 5), ("gb", 1, 6), ("x1", 0, 1, 1, 1), ("gb", 1, 7), ("head", 0),
-    ("z1", 0, 1, 2, 0), ("z1", 0, -1, 2, 0), ("x1", 0, -1, 1, 0), ("y1", 0, 1, 1, 0), ("y1", 0, -1, 1, 0),
-    ("z1", 1, 1, 1, 0), ("z1", 1, -1, 1, 0), ("z1", 1, 1, 1, 1), ("z1", 1, -1, 1, 1), ("head", 1),
-    ("x1", 0, -1, 1, 1), ("y1", 0, 1, 1, 1), ("y1", 0, -1, 1, 1), ("z1", 0, 1, 2, 1), ("x1", 1, -1, 1, 0),
-    ("z1", 0, -1, 2, 1), ("y1", 1, 1, 1, 0), ("y1", 1, -1, 1, 0), ("head", 2), ("x1", 1, -1, 1, 1),
-    ("y1", 1, 1, 1, 1), ("y1", 1, -1, 1, 1), ("x1", 1, 1, 1, 0), ("z1", 0, 1, 3, 0), ("x1", 1, 1, 1, 1),
-    ("z1", 0, -1, 3, 0), ("head", 3), ("head", 4), ("z1", 1, 1, 2, 0), ("z1", 1, -1, 2, 0), ("x1", 0, "fin", 0),
-    ("y1", 0, "fin", 0), ("z1", 1, 1, 2, 1), ("z1", 1, -1, 2, 1), ("head", 5), ("head", 6), ("z1", 0, 1, 3, 1),
-    ("z1", 0, -1, 3, 1), ("x1", 0, "fin", 1), ("y1", 0, "fin", 1), ("head", 7), ("z1", 0, "fin", 0),
-    ("x1", 1, "fin", 0), ("y1", 1, "fin", 0), ("sum", 0), ("z1", 1, 1, 3, 0), ("z1", 1, -1, 3, 0),
-    ("x1", 1, "fin", 1), ("y1", 1, "fin", 1), ("sum", 1), ("sum", 2), ("z1", 1, 1, 3, 1), ("z1", 1, -1, 3, 1),
-    ("sum", 3), ("sum", 4), ("sum", 5), ("sum", 6), ("sum", 7), ("z1", 0, "fin", 1), ("x2", 0), ("y2", 0),
-    ("z1", 1, "fin", 0), ("x2", 1), ("y2", 1), ("z1", 1, "fin", 1), ("z2", 0), ("x3", 0), ("z2", 1), ("z3", 0),
-    ("y3", 0), ("x3", 1), ("y3", 1), ("z3", 1),
+    ("z", 0), ("cz", 0, 1, 1, 1), ("cz", 0, 1, -1, 1), ("y", 0), ("cz", 0, 3, 1, 1), ("w",),
+    ("cz", 0, 3, -1, 1), ("z", 1), ("lg", 0, "z", 0), ("cz", 0, 2, 1, 1), ("cz", 0, 2, -1, 1),
+    ("lg", 0, "z", 1), ("lg", 0, "z", 7), ("lg", 0, "y", 0), ("lg", 1, "z", 0), ("b", 0), ("turn", 0),
+    ("cz", 0, 1, 1, 2), ("cz", 0, 1, -1, 2), ("turn", 1), ("turn", 2), ("cz", 0, 3, 1, 2), ("cy", 0, 1, 1, 1),
+    ("cy", 0, 1, -1, 1), ("cz", 0, 3, -1, 2), ("turn", 3), ("cz", 1, 1, 1, 1), ("a", 0), ("cz", 1, 1, -1, 1),
+    ("turn", 4), ("cz", 1, 3, 1, 1), ("turn", 5), ("cz", 1, 3, -1, 1), ("cz", 1, 2, 1, 1), ("cy", 0, 3, 1, 1),
+    ("cy", 0, 3, -1, 1), ("lg", 1, "z", 7), ("cz", 1, 2, -1, 1), ("lg", 1, "z", 1), ("cz", 0, 2, 1, 2),
+    ("lg", 0, "z", 6), ("cz", 0, 2, -1, 2), ("lg", 0, "z", 2), ("cz", 0, 1, 1, 3), ("cy", 0, 2, 1, 1),
+    ("cy", 0, 2, -1, 1), ("lg", 0, "y", 1), ("cz", 0, 1, -1, 3), ("y", 1), ("cy", 0, 1, -1, 2),
+    ("lg", 0, "y", 3), ("cz", 0, 3, 1, 3), ("cy", 0, 1, 1, 2), ("cz", 0, 3, -1, 3), ("lg", 1, "y", 0),
+    ("cz", 1, 1, 1, 2), ("cy", 0, 3, -1, 2), ("cz", 1, 1, -1, 2), ("b", 1), ("cz", 1, 3, 1, 2), ("turn", 6),
+    ("cy", 0, 3, 1, 2), ("cz", 1, 3, -1, 2), ("turn", 7), ("cz", 1, 2, 1, 2), ("a", 1), ("cz", 1, 2, -1, 2),
+    ("lg", 1, "z", 2), ("cy", 0, 2, -1, 2), ("lg", 1, "z", 6), ("cz", 0, 2, 1, 3), ("lg", 0, "z", 5),
+    ("cy", 0, 2, 1, 2), ("cz", 0, 2, -1, 3), ("cz", 0, 1, 1, 4), ("cz", 0, 1, -1, 4), ("lg", 0, "z", 3),
+    ("cy", 1, 1, -1, 1), ("cz", 0, 3, -1, 4), ("lg", 0, "y", 2), ("cz", 0, 3, 1, 4), ("a", 0, 2),
+    ("cy", 1, 1, 1, 1), ("cz", 1, 1, -1, 3), ("turn", 8), ("cz", 1, 1, 1, 3), ("b", 0, 2), ("cy", 1, 3, -1, 1),
+    ("cz", 1, 3, -1, 3), ("lg", 0, "x"), ("cz", 1, 3, 1, 3), ("cy", 1, 3, 1, 1), ("cz", 1, 2, -1, 3),
+    ("cz", 1, 2, 1, 3), ("a", 1, 2), ("lg", 1, "z", 3), ("cy", 1, 2, -1, 1), ("cz", 0, 2, 1, 4),
+    ("cz", 0, 2, -1, 4), ("lg", 0, "z", 4), ("ls", 0), ("cy", 1, 2, 1, 1), ("b", 1, 2), ("cy", 1, 1, -1, 2),
+    ("cz", 1, 1, -1, 4), ("cy", 1, 1, 1, 2), ("cz", 1, 1, 1, 4), ("cz", 1, 3, -1, 4), ("lg", 1, "z", 5),
+    ("cy", 1, 3, -1, 2), ("lg", 1, "y", 1), ("cz", 1, 3, 1, 4), ("cz", 1, 2, -1, 4), ("lg", 1, "y", 3),
+    ("cz", 1, 2, 1, 4), ("cy", 1, 3, 1, 2), ("lg", 1, "z", 4), ("cy", 1, 2, -1, 2), ("lg", 1, "x"), ("turn", 9),
+    ("turn", 10), ("cy", 1, 2, 1, 2), ("lg", 1, "y", 2), ("ls", 1), ("turn", 11), ("sz", 0), ("turn", 12),
+    ("turn", 13), ("turn", 14), ("turn", 15), ("sz", 1), ("sxy", 0), ("gb", 0, 0), ("gb", 0, 1), ("gb", 0, 2),
+    ("gb", 0, 3), ("gb", 0, 4), ("gb", 0, 5), ("gb", 0, 6), ("gb", 0, 7), ("sxy", 1), ("gb", 1, 0),
+    ("z1", 0, 1, 1, 0), ("z1", 0, -1, 1, 0), ("x1", 0, 1, 1, 0), ("gb", 1, 1), ("gb", 1, 2), ("x1", 0, 1, 1, 1),
+    ("gb", 1, 3), ("x1", 0, 1, 1, 2), ("x1", 0, -1, 1, 0), ("gb", 1, 4), ("gb", 1, 5), ("x1", 0, 1, 1, 3),
+    ("x1", 0, -1, 1, 1), ("y1", 0, 1, 1, 0), ("y1", 0, -1, 1, 0), ("gb", 1, 6), ("z1", 1, 1, 1, 0),
+    ("z1", 1, -1, 1, 0), ("x1", 0, -1, 1, 2), ("gb", 1, 7), ("z1", 1, 1, 1, 1), ("z1", 1, -1, 1, 1),
+    ("x1", 0, -1, 1, 3), ("y1", 0, 1, 1, 1), ("y1", 0, -1, 1, 1), ("head", 0), ("x1", 0, "fin", 0), ("head", 1),
+    ("z1", 0, 1, 2, 0), ("z1", 0, -1, 2, 0), ("x1", 0, "fin", 1), ("x1", 1, 1, 1, 0), ("head", 2),
+    ("z1", 1, 1, 2, 0), ("z1", 1, -1, 2, 0), ("y1", 0, "fin", 0), ("y1", 1, 1, 1, 0), ("x1", 0, "fin", 2),
+    ("y1", 1, -1, 1, 0), ("y1", 1, 1, 1, 1), ("y1", 1, -1, 1, 1), ("y1", 1, 1, 1, 2), ("y1", 1, -1, 1, 2),
+    ("y1", 1, 1, 1, 3), ("z1", 1, 1, 2, 1), ("z1", 1, -1, 2, 1), ("y1", 1, -1, 1, 3), ("x1", 1, -1, 1, 0),
+    ("head", 3), ("x1", 0, "fin", 3), ("head", 4), ("z1", 0, 1, 3, 0), ("z1", 0, -1, 3, 0), ("y1", 0, "fin", 1),
+    ("y1", 1, "fin", 0), ("head", 5), ("z1", 1, 1, 3, 0), ("z1", 1, -1, 3, 0), ("y1", 1, "fin", 1),
+    ("y1", 1, "fin", 2), ("head", 6), ("z1", 1, 1, 3, 1), ("z1", 1, -1, 3, 1), ("y1", 1, "fin", 3),
+    ("x1", 1, "fin", 0), ("head", 7), ("sum", 0), ("sum", 1), ("sum", 2), ("z1", 0, "fin", 0), ("x2", 0),
+    ("y2", 0), ("sum", 3), ("z1", 1, "fin", 0), ("sum", 4), ("sum", 5), ("sum", 6), ("y2", 1), ("x2", 1),
+    ("z1", 1, "fin", 1), ("sum", 7), ("z2", 0), ("x3", 0), ("y3", 0), ("y3", 1), ("z2", 1), ("x3", 1),
 )
 RANK = {key: i for i, key in enumerate(ORDER)}
 
@@ -75,26 +79,30 @@
     out = dict(
         hid=((CAP, D), BF16), gain=((EXITS, D), F32), n_all=((NX, CAP, D), BF16), w_all=((D, 2 * VW), BF16), w_t=((2 * VW, D), BF16),
         logit=((NX, CAP, 2 * VW), F32), dl=((NX, CAP, 2 * VW), BF16),
-        s1=((2, NZ, 2, 8, 128), F32), s2=((2, NX * NY, 2, 8, 128), F32),
+        s1=((2, NZ, 8, 128), F32), s2=((2, NX * NY, 8, 128), F32),
         st=((2, 3, 8, 128), F32), ids=((2, 8, 128), F32), loss=((2, 8, 128), F32), dn=((CAP, VW), F32),
         mine=((D, VW), F32), gs=((D, VW), BF16), gr=((D, VW), BF16),
     )
     for h in range(2):
         lx, lz, ly = [p[2] for p in PARTS[h]]
+        out[f"ownz{h}"] = ((HALVES[h][1], WIDTHS[h][0]), BF16)
+        out[f"owny{h}"] = ((HALVES[h][1], WIDTHS[h][1]), BF16)
         out[f"px{h}"] = ((NX, NZ, NY, 16, lx), BF16)
         out[f"pz{h}"] = ((NZ, NX, NY, 16, lz), BF16)
         out[f"py{h}"] = ((NY, NX, NZ, 16, ly), BF16)
-        out[f"ax{h}"] = ((2, 2, 4, 2, 16, lx), BF16)
-        out[f"bx{h}"] = ((2, 2, 1, NZ, 2, 16, lx), BF16)
-        out[f"az{h}"] = ((2, 2, 2, 2, 16, lz), BF16)
-        out[f"bz{h}"] = ((2, 2, 3, NX, 2, 16, lz), BF16)
-        out[f"ay{h}"] = ((2, 2, 2, 4, 16, ly), BF16)
-        out[f"by{h}"] = ((2, 2, 1, NX, 4, 16, ly), BF16)
+        cx, cz, cy = CHAINS[h]
+        out[f"ax{h}"] = ((2, cx, 4, NY // cx, 16, lx), BF16)
+        out[f"bx{h}"] = ((2, cx, 1, NZ, NY // cx, 16, lx), BF16)
+        out[f"az{h}"] = ((2, cz, 2, NY // cz, 16, lz), BF16)
+        out[f"bz{h}"] = ((2, cz, 3, NX, NY // cz, 16, lz), BF16)
+        out[f"ay{h}"] = ((2, cy, 2, NZ // cy, 16, ly), BF16)
+        out[f"by{h}"] = ((2, cy, 1, NX, NZ // cy, 16, ly), BF16)
         out[f"cx{h}"] = ((NY - 1, NZ, 16, lx), BF16)
-        out[f"cz{h}"] = ((NY - 1, NX, 16, lz), BF16)
+        if h not in Z_AT_ONCE:
+            out[f"cz{h}"] = ((NY - 1, NX, 16, lz), BF16)
         out[f"cy{h}"] = ((NX - 1, NZ, 16, ly), BF16)
         out[f"ex{h}"] = ((NZ - 1, 16, lx), BF16)
-        out[f"ez{h}"] = ((NX - 1, 16, lz), BF16)
+        out[f"ez{h}"] = (((NX * NY if h in Z_AT_ONCE else NX) - 1, 16, lz), BF16)
         out[f"ey{h}"] = ((NZ - 1, 16, ly), BF16)
     return out
 
@@ -160,8 +168,7 @@
 
     barrier = pltpu.get_barrier_semaphore()
     friends = [dict(dc=1)]
-    friends += [dict(dz=i) for i in range(1, NZ)]
-    friends += [dict(dx=i, dy=j) for i in range(NX) for j in range(NY) if i or j]
+    friends += [dict(dx=i) for i in range(1, NX)] + [{a: i} for a in ("dy", "dz") for i in (1, -1)]
     for f in friends:
         pl.semaphore_signal(barrier, inc=1, device_id=dev(**f), device_id_type=MESH)
     own_w = pl.ds(pl.multiple_of(c * VW, VW), VW)
@@ -226,8 +233,6 @@
         return carry
 
     loads[1].wait()
-    lax.fori_loop(0, D // 512, norm_chunk, 0)
-    pl.semaphore_wait(barrier, len(friends))
 
     def columns(h, tag, d=0):
         zw, yw, bw, aw = WIDTHS[h]
@@ -239,7 +244,7 @@
 
     def own_x(tag, h):
         rows, cols, far = pl.ds(*HALVES[h][:2]), columns(h, tag), tag in "zy"
-        src = n_all.at[0, rows, cols]
+        src = b[f"own{tag}{h}"] if far else n_all.at[0, rows, cols]
         k = slot()
         send(src, n_all.at[3, rows, cols], dev(dx=1), k)
         send(src, n_all.at[1, rows, cols], dev(dx=-1), k)
@@ -282,8 +287,8 @@
             dst = n_all.at[2, rows, cols]
             cps[tag, h, 2] = send(n_all.at[rel, rows, cols], dst, dev(dx=dx)), dst
 
-        own_rest = [lambda: own_x("b", h), lambda: own_x("a", h)]
-        for tag, n, axis, more in (("z", NZ, "dz", []), ("y", NY, "dy", own_rest)):
+        for tag, n, axis in (("z", NZ, "dz"), ("y", NY, "dy")):
+            more = [lambda k=k: own_x(*k) for k in AFTER.get((tag, h), ())]
             at((tag, h), got, tag, [chain(tag, h, n, axis, rel) for rel in (1, 3, 2)] + more)
             for d in range(n):
                 at(("lg", h, tag, d), logits, h, tag, d)
@@ -308,9 +313,22 @@
         f = pl.ds(i * 512, 512)
         w_t[:, f] = jnp.transpose(w_all[f, :], (1, 0))
 
+    def own_first(tag, h):
+        (r0, n, _), cols = HALVES[h], columns(h, tag)
+        rows = pl.ds(r0, n)
+        xs = hid[rows, cols].astype(F32)
+        g = jnp.broadcast_to(gain[0:1, cols], xs.shape)
+        for i in range(1, EXITS):
+            g = jnp.where(own_exit[r0 : r0 + n] == float(i), gain[i : i + 1, cols], g)
+        b[f"own{tag}{h}"][...] = (xs * rinv[r0 : r0 + n] * g).astype(BF16)
+
     for h in range(2):
-        own_x("z", h)
-        own_x("y", h)
+        for tag in "zy":
+            own_first(tag, h)
+    pl.semaphore_wait(barrier, len(friends))
+    for tag, h in FIRST:
+        own_x(tag, h)
+    lax.fori_loop(0, D // 512, norm_chunk, 0)
     for h in range(2):
         gather(h)
     loads[2].wait()
@@ -359,28 +377,35 @@
             for i in range(4):
                 row = jnp.broadcast_to(to_row(values[i], r0), (8, 128))
                 stats[i] = jnp.where(here, row, stats[i])
-        s1[h, z, 0] = jnp.where(upper, stats[0], pltpu.roll(stats[1], 4, 0))
-        s1[h, z, 1] = jnp.where(upper, stats[2], pltpu.roll(stats[3], 4, 0))
+        first = jnp.where(upper, stats[0], pltpu.roll(stats[1], 4, 0))
+        rest = jnp.where(upper, stats[2], pltpu.roll(stats[3], 4, 0))
+        s1[h, z] = jnp.where(mine_lanes(h), first, pltpu.roll(rest, 64, 1))
         cps["s1", h] = slot()
         for i in range(1, NZ):
             send(s1.at[h, z], s1.at[h, z], dev(dz=i), cps["s1", h])
 
-    def merge(ref, n):
-        first = [ref[q, 0] for q in range(n)]
-        peaks = [jnp.where(upper, a, pltpu.roll(a, 4, 0)) for a in first]
+    def mine_lanes(h):
+        r0, n, _ = HALVES[h]
+        return (lane >= r0) & (lane < r0 + n)
+
+    def merge(h, ref, n):
+        own_lanes = mine_lanes(h)
+        sets = [ref[q] for q in range(n)]
+        peaks = [jnp.where(upper, a, pltpu.roll(a, 4, 0)) for a in sets]
         peak = peaks[0]
         for p in peaks[1:]:
             peak = jnp.maximum(peak, p)
-        f = [jnp.exp(p - peak) for p in peaks]
-        total = sum(a * g for a, g in zip(first, f))
-        rest = sum(ref[q, 1] * jnp.where(upper, f[q], 1.0) for q in range(n))
-        return jnp.where(upper, peak, total), rest
+        total = jnp.zeros((8, 128), F32)
+        for a, p in zip(sets, peaks):
+            f = jnp.exp(p - peak)
+            total = total + a * jnp.where(own_lanes, f, jnp.where(upper, pltpu.roll(f, 64, 1), 1.0))
+        return jnp.where(own_lanes & upper, peak, total)
 
     own = x * NY + y
 
     def stats_z(h):
         arrived(cps["s1", h], s1.at[h, 0 : NZ - 1])
-        s2[h, own, 0], s2[h, own, 1] = merge(s1.at[h], NZ)
+        s2[h, own] = merge(h, s1.at[h], NZ)
         cps["s2", h] = slot()
         for i in range(NX):
             for j in range(NY):
@@ -391,7 +416,8 @@
 
     def stats_xy(h):
         arrived(cps["s2", h], s2.at[h, 0 : NX * NY - 1])
-        peak, mean = merge(s2.at[h], NX * NY)
+        peak = merge(h, s2.at[h], NX * NY)
+        mean = pltpu.roll(peak, 64, 1)
         total, chosen = pltpu.roll(peak, 4, 0), pltpu.roll(mean, 4, 0)
         lse = peak + jnp.log(total)
         weight = st[h, 1]
@@ -438,13 +464,13 @@
 
         lax.fori_loop(0, dst.shape[0], one, 0)
 
-    def ring(tag, h, n, axis, block, one_way, buf_a, buf_b, done):
+    def ring(tag, h, n, axis, n_chains, block, one_way, buf_a, buf_b, done):
         half = n // 2
         side = {1: 0, -1: 1}
-        left = [2]
+        left = [n_chains]
 
         def begin(sign):
-            for i in range(2):
+            for i in range(n_chains):
                 src = one_way(block(half, i), sign)
                 cps[tag, h, sign, 1, i] = send(src, buf_a.at[side[sign], i], dev(**{axis: sign}))
 
@@ -468,10 +494,10 @@
                 done()
 
         for k in range(1, half):
-            for i in range(2):
+            for i in range(n_chains):
                 for sign in (1, -1):
                     at((tag, h, sign, k, i), arrive, sign, k, i)
-        for i in range(2):
+        for i in range(n_chains):
             at((tag, h, "fin", i), finish, i)
         return begin
 
@@ -491,8 +517,27 @@
         at((tag, h), finish)
         return begin
 
+    def direct2(tag, h, axes, sizes, block, buf, done):
+        pairs = [(i, j) for i in range(sizes[0]) for j in range(sizes[1]) if i or j]
+
+        def begin():
+            cps[tag, h] = slot()
+            for q, (i, j) in enumerate(pairs):
+                send(block(i, j), buf.at[q], dev(**{axes[0]: i, axes[1]: j}), cps[tag, h])
+
+        def finish():
+            arrived(cps[tag, h], buf)
+            acc = block(0, 0)[...].astype(F32)
+            for q in range(len(pairs)):
+                acc = acc + buf[q].astype(F32)
+            done(acc)
+
+        at((tag, h), finish)
+        return begin
+
     def reduce(h):
         px, pz, py = b[f"px{h}"], b[f"pz{h}"], b[f"py{h}"]
+        cx, cz, cy = CHAINS[h]
 
         def put(i):
             r, l, w = PARTS[h][i]
@@ -511,15 +556,18 @@
 
         x3 = direct("x3", h, NZ, "dz", lambda d: px.at[0, ZPOS[d], 0], b[f"ex{h}"], put(0))
         x2 = direct("x2", h, NY, "dy", lambda d: px.at[0, :, d], b[f"cx{h}"], back(px.at[0, :, 0], x3))
-        x1 = ring("x1", h, NX, "dx", lambda d, i: px.at[d, :, 2 * i : 2 * i + 2], cut(4),
+        x1 = ring("x1", h, NX, "dx", cx, lambda d, i: px.at[d, :, i * NY // cx : (i + 1) * NY // cx], cut(4),
                   b[f"ax{h}"], b[f"bx{h}"], x2)
-        z3 = direct("z3", h, NX, "dx", lambda d: pz.at[7, d, 0], b[f"ez{h}"], put(1))
-        z2 = direct("z2", h, NY, "dy", lambda d: pz.at[7, :, d], b[f"cz{h}"], back(pz.at[7, :, 0], z3))
-        z1 = ring("z1", h, NZ, "dz", lambda d, i: pz.at[ZPOS[d], :, 2 * i : 2 * i + 2], cut(2),
+        if h in Z_AT_ONCE:
+            z2 = direct2("z2", h, ("dy", "dx"), (NY, NX), lambda i, j: pz.at[7, j, i], b[f"ez{h}"], put(1))
+        else:
+            z3 = direct("z3", h, NX, "dx", lambda d: pz.at[7, d, 0], b[f"ez{h}"], put(1))
+            z2 = direct("z2", h, NY, "dy", lambda d: pz.at[7, :, d], b[f"cz{h}"], back(pz.at[7, :, 0], z3))
+        z1 = ring("z1", h, NZ, "dz", cz, lambda d, i: pz.at[ZPOS[d], :, i * NY // cz : (i + 1) * NY // cz], cut(2),
                   b[f"az{h}"], b[f"bz{h}"], z2)
         y3 = direct("y3", h, NZ, "dz", lambda d: py.at[0, 0, ZPOS[d]], b[f"ey{h}"], put(2))
         y2 = direct("y2", h, NX, "dx", lambda d: py.at[0, d], b[f"cy{h}"], back(py.at[0, 0], y3))
-        y1 = ring("y1", h, NY, "dy", lambda d, i: py.at[d, :, 4 * i : 4 * i + 4], cut(2),
+        y1 = ring("y1", h, NY, "dy", cy, lambda d, i: py.at[d, :, i * NZ // cy : (i + 1) * NZ // cy], cut(2),
                   b[f"ay{h}"], b[f"by{h}"], y2)
         then = {
             0: (lambda: z1(1), lambda: z1(-1)),

time: 82.5 us -> 79.1 us (0.959)
  Pallas kernels: 80.8 us -> 78 us
    pallas_call x1, Pallas kernels: 77 us -> 74.2 us  [body(): pl.pallas_call(kernel, out_shape=(jax.ShapeDtypeStruct((8, 128), F32), bi...]
where the time goes in v5:
time: 79.1 us; the launch traced here: 78.8 us
  Pallas kernels  78 us (99%)
  between operations  0.8 us (1%)
    pallas_call x1, Pallas kernels, body(): pl.pallas_call(kernel, out_shape=(jax.ShapeDtypeStruct((8, 128), F32), bi...  74.2 us
    pallas_call x1, Pallas kernels, body(): pl.pallas_call(handover, out_shape=(jax.ShapeDtypeStruct((1, 1), F32), bi...  3.84 us

profile of v5, /device:TPU:2, one launch (start us, length us, event | category | flops | bytes accessed | tf_op | source)
XLA Modules:
  0.0 78.8 jit_solution(8622606081617675823)
XLA Ops:
  0.6 74.2 %exit_head.1 = (f32[8,128]{1,0:T(8,128)}, bf16[8192,256]{1,0:T(8,128)(2,1)}, bf16[80,256]{1,0:T(8,128)(2,1)}) custom-call(bf16[80,8192]{1,0:T(8,128)(2,1)} %hidden.1, f32[4,8192]{1,0:T(4,128)} %gain_in.1, bf16[8192,256]{1,0:T(8,128)(2,1)} %head.1, s32[640]{0:T(1024)} %targets.1, s32[640]{0:T(1024)} %exit_ids.1, s32[8]{0:T(128)} %counts.1, f32[4]{0:T(128)} %scale.1), custom_call_target="tpu_custom_call" | custom-call | tf_op jit(solution)/shard_map/exit_head/pallas_call | solution.py:656
  74.8 3.8 %handover.1 = (f32[1,1]{1,0:T(1,128)}, bf16[8192,256]{1,0:T(8,128)(2,1)}, bf16[80,256]{1,0:T(8,128)(2,1)}) custom-call(f32[8,128]{1,0:T(8,128)} %get-tuple-element.9.loss, bf16[8192,256]{1,0:T(8,128)(2,1)} %get-tuple-element.10.grad_weight, bf16[80,256]{1,0:T(8,128)(2,1)} %get-tuple-element.11.grad_hidden), custom_call_target="tpu_custom_call" | custom-call | tf_op jit(solution)/shard_map/handover/pallas_call | solution.py:667

commit v6 on v5

--- a/solution.py
+++ b/solution.py
@@ -22,7 +22,7 @@
 ZORD = (4, 3, 5, 2, 6, 1, 7, 0)
 ZPOS = {d: k for k, d in enumerate(ZORD)}
 N_SEND = 40
-N_RECV = 176
+N_RECV = 180
 HALVES = ((0, 48, 32), (48, 32, 16))
 PARTS = (((0, 0, 256), (16, 0, 256), (32, 0, 256)), ((48, 0, 128), (64, 0, 256), (48, 128, 128)))
 FIRST = (('z', 0), ('y', 0), ('z', 1))
@@ -31,46 +31,47 @@
 Z_AT_ONCE = (0, 1)
 TN = (((0,), (0,)), ((), ()))
 ORDER = (
-    ("z", 0), ("cz", 0, 1, 1, 1), ("cz", 0, 1, -1, 1), ("y", 0), ("cz", 0, 3, 1, 1), ("w",),
-    ("cz", 0, 3, -1, 1), ("z", 1), ("lg", 0, "z", 0), ("cz", 0, 2, 1, 1), ("cz", 0, 2, -1, 1),
-    ("lg", 0, "z", 1), ("lg", 0, "z", 7), ("lg", 0, "y", 0), ("lg", 1, "z", 0), ("b", 0), ("turn", 0),
-    ("cz", 0, 1, 1, 2), ("cz", 0, 1, -1, 2), ("turn", 1), ("turn", 2), ("cz", 0, 3, 1, 2), ("cy", 0, 1, 1, 1),
-    ("cy", 0, 1, -1, 1), ("cz", 0, 3, -1, 2), ("turn", 3), ("cz", 1, 1, 1, 1), ("a", 0), ("cz", 1, 1, -1, 1),
-    ("turn", 4), ("cz", 1, 3, 1, 1), ("turn", 5), ("cz", 1, 3, -1, 1), ("cz", 1, 2, 1, 1), ("cy", 0, 3, 1, 1),
-    ("cy", 0, 3, -1, 1), ("lg", 1, "z", 7), ("cz", 1, 2, -1, 1), ("lg", 1, "z", 1), ("cz", 0, 2, 1, 2),
-    ("lg", 0, "z", 6), ("cz", 0, 2, -1, 2), ("lg", 0, "z", 2), ("cz", 0, 1, 1, 3), ("cy", 0, 2, 1, 1),
-    ("cy", 0, 2, -1, 1), ("lg", 0, "y", 1), ("cz", 0, 1, -1, 3), ("y", 1), ("cy", 0, 1, -1, 2),
-    ("lg", 0, "y", 3), ("cz", 0, 3, 1, 3), ("cy", 0, 1, 1, 2), ("cz", 0, 3, -1, 3), ("lg", 1, "y", 0),
-    ("cz", 1, 1, 1, 2), ("cy", 0, 3, -1, 2), ("cz", 1, 1, -1, 2), ("b", 1), ("cz", 1, 3, 1, 2), ("turn", 6),
-    ("cy", 0, 3, 1, 2), ("cz", 1, 3, -1, 2), ("turn", 7), ("cz", 1, 2, 1, 2), ("a", 1), ("cz", 1, 2, -1, 2),
-    ("lg", 1, "z", 2), ("cy", 0, 2, -1, 2), ("lg", 1, "z", 6), ("cz", 0, 2, 1, 3), ("lg", 0, "z", 5),
-    ("cy", 0, 2, 1, 2), ("cz", 0, 2, -1, 3), ("cz", 0, 1, 1, 4), ("cz", 0, 1, -1, 4), ("lg", 0, "z", 3),
-    ("cy", 1, 1, -1, 1), ("cz", 0, 3, -1, 4), ("lg", 0, "y", 2), ("cz", 0, 3, 1, 4), ("a", 0, 2),
-    ("cy", 1, 1, 1, 1), ("cz", 1, 1, -1, 3), ("turn", 8), ("cz", 1, 1, 1, 3), ("b", 0, 2), ("cy", 1, 3, -1, 1),
-    ("cz", 1, 3, -1, 3), ("lg", 0, "x"), ("cz", 1, 3, 1, 3), ("cy", 1, 3, 1, 1), ("cz", 1, 2, -1, 3),
-    ("cz", 1, 2, 1, 3), ("a", 1, 2), ("lg", 1, "z", 3), ("cy", 1, 2, -1, 1), ("cz", 0, 2, 1, 4),
-    ("cz", 0, 2, -1, 4), ("lg", 0, "z", 4), ("ls", 0), ("cy", 1, 2, 1, 1), ("b", 1, 2), ("cy", 1, 1, -1, 2),
-    ("cz", 1, 1, -1, 4), ("cy", 1, 1, 1, 2), ("cz", 1, 1, 1, 4), ("cz", 1, 3, -1, 4), ("lg", 1, "z", 5),
-    ("cy", 1, 3, -1, 2), ("lg", 1, "y", 1), ("cz", 1, 3, 1, 4), ("cz", 1, 2, -1, 4), ("lg", 1, "y", 3),
-    ("cz", 1, 2, 1, 4), ("cy", 1, 3, 1, 2), ("lg", 1, "z", 4), ("cy", 1, 2, -1, 2), ("lg", 1, "x"), ("turn", 9),
-    ("turn", 10), ("cy", 1, 2, 1, 2), ("lg", 1, "y", 2), ("ls", 1), ("turn", 11), ("sz", 0), ("turn", 12),
-    ("turn", 13), ("turn", 14), ("turn", 15), ("sz", 1), ("sxy", 0), ("gb", 0, 0), ("gb", 0, 1), ("gb", 0, 2),
-    ("gb", 0, 3), ("gb", 0, 4), ("gb", 0, 5), ("gb", 0, 6), ("gb", 0, 7), ("sxy", 1), ("gb", 1, 0),
-    ("z1", 0, 1, 1, 0), ("z1", 0, -1, 1, 0), ("x1", 0, 1, 1, 0), ("gb", 1, 1), ("gb", 1, 2), ("x1", 0, 1, 1, 1),
-    ("gb", 1, 3), ("x1", 0, 1, 1, 2), ("x1", 0, -1, 1, 0), ("gb", 1, 4), ("gb", 1, 5), ("x1", 0, 1, 1, 3),
-    ("x1", 0, -1, 1, 1), ("y1", 0, 1, 1, 0), ("y1", 0, -1, 1, 0), ("gb", 1, 6), ("z1", 1, 1, 1, 0),
-    ("z1", 1, -1, 1, 0), ("x1", 0, -1, 1, 2), ("gb", 1, 7), ("z1", 1, 1, 1, 1), ("z1", 1, -1, 1, 1),
-    ("x1", 0, -1, 1, 3), ("y1", 0, 1, 1, 1), ("y1", 0, -1, 1, 1), ("head", 0), ("x1", 0, "fin", 0), ("head", 1),
-    ("z1", 0, 1, 2, 0), ("z1", 0, -1, 2, 0), ("x1", 0, "fin", 1), ("x1", 1, 1, 1, 0), ("head", 2),
-    ("z1", 1, 1, 2, 0), ("z1", 1, -1, 2, 0), ("y1", 0, "fin", 0), ("y1", 1, 1, 1, 0), ("x1", 0, "fin", 2),
-    ("y1", 1, -1, 1, 0), ("y1", 1, 1, 1, 1), ("y1", 1, -1, 1, 1), ("y1", 1, 1, 1, 2), ("y1", 1, -1, 1, 2),
-    ("y1", 1, 1, 1, 3), ("z1", 1, 1, 2, 1), ("z1", 1, -1, 2, 1), ("y1", 1, -1, 1, 3), ("x1", 1, -1, 1, 0),
-    ("head", 3), ("x1", 0, "fin", 3), ("head", 4), ("z1", 0, 1, 3, 0), ("z1", 0, -1, 3, 0), ("y1", 0, "fin", 1),
-    ("y1", 1, "fin", 0), ("head", 5), ("z1", 1, 1, 3, 0), ("z1", 1, -1, 3, 0), ("y1", 1, "fin", 1),
-    ("y1", 1, "fin", 2), ("head", 6), ("z1", 1, 1, 3, 1), ("z1", 1, -1, 3, 1), ("y1", 1, "fin", 3),
-    ("x1", 1, "fin", 0), ("head", 7), ("sum", 0), ("sum", 1), ("sum", 2), ("z1", 0, "fin", 0), ("x2", 0),
-    ("y2", 0), ("sum", 3), ("z1", 1, "fin", 0), ("sum", 4), ("sum", 5), ("sum", 6), ("y2", 1), ("x2", 1),
-    ("z1", 1, "fin", 1), ("sum", 7), ("z2", 0), ("x3", 0), ("y3", 0), ("y3", 1), ("z2", 1), ("x3", 1),
+    ("z", 0), ("z", 0, "far"), ("y", 0), ("cz", 0, 1, 1, 1), ("cz", 0, 1, -1, 1), ("cz", 0, 3, 1, 1),
+    ("cz", 0, 3, -1, 1), ("z", 1), ("y", 0, "far"), ("cz", 0, 2, 1, 1), ("cz", 0, 2, -1, 1), ("w",),
+    ("z", 1, "far"), ("lg", 0, "z", 0), ("lg", 0, "z", 1), ("cz", 0, 1, 1, 2), ("cz", 0, 1, -1, 2),
+    ("cy", 0, 1, 1, 1), ("cy", 0, 1, -1, 1), ("lg", 0, "z", 7), ("lg", 0, "y", 0), ("cz", 0, 3, 1, 2),
+    ("cz", 0, 3, -1, 2), ("lg", 1, "z", 0), ("b", 0), ("cz", 1, 1, 1, 1), ("cz", 1, 1, -1, 1), ("turn", 0),
+    ("cy", 0, 3, 1, 1), ("cy", 0, 3, -1, 1), ("turn", 1), ("cz", 1, 3, 1, 1), ("cz", 1, 3, -1, 1), ("turn", 2),
+    ("cz", 0, 2, 1, 2), ("cz", 0, 2, -1, 2), ("lg", 0, "z", 2), ("lg", 0, "z", 6), ("a", 0), ("cz", 1, 2, 1, 1),
+    ("cz", 1, 2, -1, 1), ("cy", 0, 2, 1, 1), ("cy", 0, 2, -1, 1), ("lg", 0, "y", 1), ("cy", 0, 1, -1, 2),
+    ("cz", 0, 1, 1, 3), ("cz", 0, 1, -1, 3), ("lg", 0, "y", 3), ("y", 1), ("cy", 0, 1, 1, 2), ("lg", 1, "z", 1),
+    ("cy", 0, 3, -1, 2), ("cz", 0, 3, 1, 3), ("cz", 0, 3, -1, 3), ("lg", 1, "z", 7), ("turn", 3),
+    ("cz", 1, 1, 1, 2), ("cz", 1, 1, -1, 2), ("cy", 0, 3, 1, 2), ("y", 1, "far"), ("lg", 1, "y", 0),
+    ("cz", 1, 3, 1, 2), ("cz", 1, 3, -1, 2), ("turn", 4), ("cy", 0, 2, -1, 2), ("cz", 0, 2, 1, 3),
+    ("cz", 0, 2, -1, 3), ("lg", 0, "z", 3), ("cy", 0, 2, 1, 2), ("lg", 0, "z", 5), ("b", 1), ("cz", 1, 2, 1, 2),
+    ("cz", 1, 2, -1, 2), ("cz", 0, 1, -1, 4), ("lg", 0, "y", 2), ("cz", 0, 1, 1, 4), ("cz", 0, 3, -1, 4),
+    ("cy", 1, 1, 1, 1), ("cy", 1, 1, -1, 1), ("a", 1), ("lg", 1, "z", 2), ("cz", 0, 3, 1, 4), ("lg", 1, "z", 6),
+    ("cz", 1, 1, -1, 3), ("cz", 1, 1, 1, 3), ("turn", 5), ("cy", 1, 3, 1, 1), ("cy", 1, 3, -1, 1),
+    ("cz", 1, 3, -1, 3), ("turn", 6), ("cz", 1, 3, 1, 3), ("cz", 0, 2, -1, 4), ("turn", 7), ("cz", 0, 2, 1, 4),
+    ("a", 0, 2), ("cy", 1, 2, 1, 1), ("cy", 1, 2, -1, 1), ("lg", 0, "z", 4), ("cz", 1, 2, -1, 3),
+    ("cz", 1, 2, 1, 3), ("b", 0, 2), ("lg", 0, "x"), ("ls", 0), ("cy", 1, 1, 1, 2), ("cy", 1, 1, -1, 2),
+    ("a", 1, 2), ("cz", 1, 1, -1, 4), ("cz", 1, 1, 1, 4), ("cz", 1, 3, -1, 4), ("cy", 1, 3, 1, 2),
+    ("cy", 1, 3, -1, 2), ("cz", 1, 3, 1, 4), ("b", 1, 2), ("lg", 1, "z", 3), ("lg", 1, "z", 5),
+    ("cy", 1, 2, 1, 2), ("cy", 1, 2, -1, 2), ("lg", 1, "y", 1), ("cz", 1, 2, -1, 4), ("cz", 1, 2, 1, 4),
+    ("lg", 1, "z", 4), ("lg", 1, "y", 2), ("lg", 1, "y", 3), ("lg", 1, "x"), ("ls", 1), ("sz", 0), ("turn", 8),
+    ("turn", 9), ("turn", 10), ("turn", 11), ("turn", 12), ("turn", 13), ("turn", 14), ("turn", 15), ("sz", 1),
+    ("sxy", 0), ("gb", 0, 0), ("gb", 0, 1), ("gb", 0, 2), ("gb", 0, 3), ("gb", 0, 4), ("gb", 0, 5),
+    ("gb", 0, 6), ("gb", 0, 7), ("sxy", 1), ("gb", 1, 0), ("z1", 0, 1, 1, 0), ("z1", 0, -1, 1, 0),
+    ("x1", 0, 1, 1, 0), ("gb", 1, 1), ("gb", 1, 2), ("x1", 0, 1, 1, 1), ("gb", 1, 3), ("gb", 1, 4),
+    ("x1", 0, 1, 1, 2), ("x1", 0, -1, 1, 0), ("gb", 1, 5), ("x1", 0, 1, 1, 3), ("x1", 0, -1, 1, 1),
+    ("y1", 0, 1, 1, 0), ("y1", 0, -1, 1, 0), ("gb", 1, 6), ("z1", 1, 1, 1, 0), ("z1", 1, -1, 1, 0),
+    ("x1", 0, -1, 1, 2), ("gb", 1, 7), ("z1", 1, 1, 1, 1), ("z1", 1, -1, 1, 1), ("x1", 0, -1, 1, 3),
+    ("y1", 0, 1, 1, 1), ("y1", 0, -1, 1, 1), ("head", 0), ("head", 1), ("x1", 0, "fin", 0), ("z1", 0, 1, 2, 0),
+    ("z1", 0, -1, 2, 0), ("x1", 1, 1, 1, 0), ("x1", 0, "fin", 1), ("head", 2), ("z1", 1, 1, 2, 0),
+    ("z1", 1, -1, 2, 0), ("y1", 0, "fin", 0), ("y1", 1, 1, 1, 0), ("y1", 1, -1, 1, 0), ("x1", 0, "fin", 2),
+    ("y1", 1, 1, 1, 1), ("y1", 1, -1, 1, 1), ("y1", 1, 1, 1, 2), ("y1", 1, -1, 1, 2), ("y1", 1, 1, 1, 3),
+    ("z1", 1, 1, 2, 1), ("z1", 1, -1, 2, 1), ("y1", 1, -1, 1, 3), ("x1", 1, -1, 1, 0), ("head", 3), ("head", 4),
+    ("x1", 0, "fin", 3), ("z1", 0, 1, 3, 0), ("z1", 0, -1, 3, 0), ("y1", 0, "fin", 1), ("y1", 1, "fin", 0),
+    ("head", 5), ("z1", 1, 1, 3, 0), ("z1", 1, -1, 3, 0), ("y1", 1, "fin", 1), ("y1", 1, "fin", 2), ("head", 6),
+    ("z1", 1, 1, 3, 1), ("z1", 1, -1, 3, 1), ("y1", 1, "fin", 3), ("x1", 1, "fin", 0), ("head", 7), ("sum", 0),
+    ("sum", 1), ("sum", 2), ("z1", 0, "fin", 0), ("x2", 0), ("y2", 0), ("sum", 3), ("z1", 1, "fin", 0),
+    ("sum", 4), ("sum", 5), ("sum", 6), ("y2", 1), ("x2", 1), ("z1", 1, "fin", 1), ("sum", 7), ("z2", 0),
+    ("x3", 0), ("y3", 0), ("y3", 1), ("z2", 1), ("x3", 1),
 )
 RANK = {key: i for i, key in enumerate(ORDER)}
 
@@ -173,7 +174,10 @@
         pl.semaphore_signal(barrier, inc=1, device_id=dev(**f), device_id_type=MESH)
     own_w = pl.ds(pl.multiple_of(c * VW, VW), VW)
     loads = [
-        pltpu.make_async_copy(hidden, hid, lsem.at[0]),
+        pltpu.make_async_copy(hidden.at[:, cols], hid.at[:, cols], lsem.at[11 + i])
+        for i, cols in enumerate(pl.ds(i * D // 4, D // 4) for i in range(4))
+    ]
+    loads += [
         pltpu.make_async_copy(gain_in, gain, lsem.at[1]),
         pltpu.make_async_copy(head, w_all.at[:, own_w], lsem.at[2]),
     ]
@@ -222,8 +226,10 @@
             acc = acc + xs[:, j * 128 : (j + 1) * 128]
         return acc
 
-    loads[0].wait()
-    total_sq = lax.fori_loop(0, D // 512, squares, jnp.zeros((CAP, 128), F32))
+    total_sq = jnp.zeros((CAP, 128), F32)
+    for i in range(4):
+        loads[i].wait()
+        total_sq = lax.fori_loop(4 * i, 4 * i + 4, squares, total_sq)
     rinv = lax.rsqrt(jnp.sum(total_sq, axis=1, keepdims=True) / D + 1e-05)
 
     def norm_chunk(i, carry):
@@ -232,7 +238,7 @@
         n_all[0, :, cols] = (xs * rinv * gain_rows(cols, own_exit)).astype(BF16)
         return carry
 
-    loads[1].wait()
+    loads[4].wait()
 
     def columns(h, tag, d=0):
         zw, yw, bw, aw = WIDTHS[h]
@@ -248,9 +254,10 @@
         k = slot()
         send(src, n_all.at[3, rows, cols], dev(dx=1), k)
         send(src, n_all.at[1, rows, cols], dev(dx=-1), k)
+        cps[tag, h] = k, n_all.at[0:2, rows, cols]
         if far:
-            send(src, n_all.at[2, rows, cols], dev(dx=2), k)
-        cps[tag, h] = k, n_all.at[0 : 3 if far else 2, rows, cols]
+            dst = n_all.at[2, rows, cols]
+            cps[tag, h, "far"] = send(src, dst, dev(dx=2)), dst
 
     def chain(tag, h, n, axis, rel):
         half = n // 2
@@ -275,8 +282,8 @@
         return begin
 
     def gather(h):
-        def got(tag, then):
-            arrived(*cps[tag, h])
+        def got(key, then):
+            arrived(*cps[key])
             for fn in then:
                 fn()
 
@@ -289,7 +296,8 @@
 
         for tag, n, axis in (("z", NZ, "dz"), ("y", NY, "dy")):
             more = [lambda k=k: own_x(*k) for k in AFTER.get((tag, h), ())]
-            at((tag, h), got, tag, [chain(tag, h, n, axis, rel) for rel in (1, 3, 2)] + more)
+            at((tag, h), got, (tag, h), [chain(tag, h, n, axis, rel) for rel in (1, 3)] + more)
+            at((tag, h, "far"), got, (tag, h, "far"), [chain(tag, h, n, axis, 2)])
             for d in range(n):
                 at(("lg", h, tag, d), logits, h, tag, d)
         for tag in "ba":
@@ -331,7 +339,7 @@
     lax.fori_loop(0, D // 512, norm_chunk, 0)
     for h in range(2):
         gather(h)
-    loads[2].wait()
+    loads[5].wait()
     mine_w = w_all.at[:, own_w]
     cps["w"] = send(mine_w, mine_w, dev(dc=1)), mine_w
     at(("w",), take_w)
@@ -617,7 +625,7 @@
     gh_out[...] = (rinv * (scaled - unit * (inner / D))).astype(BF16)
 
     arrived(cps["loss"], loss_x.at[1])
-    loss_out[...] = (loss_x[0] + loss_x[1]) / 512.0
+    loss_out[...] = (loss_x[0, 0:1, 0:1] + loss_x[1, 0:1, 0:1]) / 512.0
     for cp in outs:
         cp.wait()
     for cp in pool:
@@ -631,18 +639,18 @@
     parts = [pl.ds(i * n, n) for i in range(4)]
     reads = [pltpu.make_async_copy(grad_weight.at[p], buf.at[p], sem.at[i]) for i, p in enumerate(parts)]
     writes = [pltpu.make_async_copy(buf.at[p], gw_out.at[p], sem.at[4 + i]) for i, p in enumerate(parts)]
-    reads += [pltpu.make_async_copy(grad_hidden, small, sem.at[8])]
-    writes += [pltpu.make_async_copy(small, gh_out, sem.at[9])]
-    get_loss = pltpu.make_async_copy(loss, total, sem.at[10])
+    extra = [
+        (pltpu.make_async_copy(grad_hidden, small, sem.at[8]), pltpu.make_async_copy(small, gh_out, sem.at[9])),
+        (pltpu.make_async_copy(loss, total, sem.at[10]), pltpu.make_async_copy(total, loss_out, sem.at[11])),
+    ]
+    for r, _ in extra:
+        r.start()
     for r in reads:
         r.start()
-    get_loss.start()
-    for r, w in zip(reads, writes):
+    for r, w in extra + list(zip(reads, writes)):
         r.wait()
         w.start()
-    get_loss.wait()
-    loss_out[...] = total[0:1, 0:1]
-    for w in writes:
+    for w in writes + [w for _, w in extra]:
         w.wait()
 
 
@@ -655,10 +663,10 @@
     small = jax.ShapeDtypeStruct((CAP, VW), BF16)
     results = pl.pallas_call(
         kernel,
-        out_shape=(jax.ShapeDtypeStruct((8, 128), F32), big, small),
+        out_shape=(jax.ShapeDtypeStruct((1, 1), F32), big, small),
         in_specs=[hbm, hbm, hbm, smem, smem, smem, smem],
         out_specs=(vmem, hbm, vmem),
-        scratch_shapes=[pltpu.VMEM(*v) for v in SCRATCH.values()] + [dma((N_SEND,)), dma((N_RECV,)), dma((11,))],
+        scratch_shapes=[pltpu.VMEM(*v) for v in SCRATCH.values()] + [dma((N_SEND,)), dma((N_RECV,)), dma((15,))],
         compiler_params=pltpu.CompilerParams(
             collective_id=0, has_side_effects=True, vmem_limit_bytes=60 * 2**20
         ),
@@ -668,9 +676,9 @@
         handover,
         out_shape=(jax.ShapeDtypeStruct((1, 1), F32), big, small),
         in_specs=[hbm, hbm, hbm],
-        out_specs=(vmem, hbm, hbm),
+        out_specs=(hbm, hbm, hbm),
         scratch_shapes=[
-            pltpu.VMEM((D, VW), BF16), pltpu.VMEM((CAP, VW), BF16), pltpu.VMEM((8, 128), F32), dma((11,)),
+            pltpu.VMEM((D, VW), BF16), pltpu.VMEM((CAP, VW), BF16), pltpu.VMEM((1, 1), F32), dma((12,)),
         ],
         compiler_params=pltpu.CompilerParams(vmem_limit_bytes=58 * 2**20),
         name="handover",

time: 79.1 us -> 78.1 us (0.987)
  Pallas kernels: 78 us -> 77.1 us
    pallas_call x1, Pallas kernels: 74.2 us -> 73.1 us  [body(): pl.pallas_call(kernel, out_shape=(jax.ShapeDtypeStruct((1, 1), F32), big,...]
where the time goes in v6:
time: 78.1 us; the launch traced here: 77.9 us
  Pallas kernels  77.1 us (99%)
  between operations  0.8 us (1%)
    pallas_call x1, Pallas kernels, body(): pl.pallas_call(kernel, out_shape=(jax.ShapeDtypeStruct((1, 1), F32), big,...  73.1 us
    pallas_call x1, Pallas kernels, body(): pl.pallas_call(handover, out_shape=(jax.ShapeDtypeStruct((1, 1), F32), bi...  4.04 us

profile of v6, /device:TPU:2, one launch (start us, length us, event | category | flops | bytes accessed | tf_op | source)
XLA Modules:
  0.0 77.9 jit_solution(8205458607676403309)
XLA Ops:
  0.6 73.1 %exit_head.1 = (f32[1,1]{1,0:T(1,128)}, bf16[8192,256]{1,0:T(8,128)(2,1)}, bf16[80,256]{1,0:T(8,128)(2,1)}) custom-call(bf16[80,8192]{1,0:T(8,128)(2,1)} %hidden.1, f32[4,8192]{1,0:T(4,128)} %gain_in.1, bf16[8192,256]{1,0:T(8,128)(2,1)} %head.1, s32[640]{0:T(1024)} %targets.1, s32[640]{0:T(1024)} %exit_ids.1, s32[8]{0:T(128)} %counts.1, f32[4]{0:T(128)} %scale.1), custom_call_target="tpu_custom_call" | custom-call | tf_op jit(solution)/shard_map/exit_head/pallas_call | solution.py:664
  73.7 4.0 %handover.1 = (f32[1,1]{1,0:T(1,128)}, bf16[8192,256]{1,0:T(8,128)(2,1)}, bf16[80,256]{1,0:T(8,128)(2,1)}) custom-call(f32[1,1]{1,0:T(1,128)} %get-tuple-element.9.loss, bf16[8192,256]{1,0:T(8,128)(2,1)} %get-tuple-element.10.grad_weight, bf16[80,256]{1,0:T(8,128)(2,1)} %get-tuple-element.11.grad_hidden), custom_call_target="tpu_custom_call" | custom-call | tf_op jit(solution)/shard_map/handover/pallas_call | solution.py:675

commit v7 on v6

--- a/solution.py
+++ b/solution.py
@@ -22,7 +22,7 @@
 ZORD = (4, 3, 5, 2, 6, 1, 7, 0)
 ZPOS = {d: k for k, d in enumerate(ZORD)}
 N_SEND = 40
-N_RECV = 180
+N_RECV = 102
 HALVES = ((0, 48, 32), (48, 32, 16))
 PARTS = (((0, 0, 256), (16, 0, 256), (32, 0, 256)), ((48, 0, 128), (64, 0, 256), (48, 128, 128)))
 FIRST = (('z', 0), ('y', 0), ('z', 1))
@@ -140,6 +140,17 @@
         slots[0] += 1
         return slots[0] - 1
 
+    gathered = ([], [])
+
+    def slot_of(h):
+        gathered[h].append(slot())
+        return gathered[h][-1]
+
+    def spare(h):
+        k = gathered[h].pop(0) if gathered[h] else slot()
+        assert k not in pending
+        return k
+
     def send(src, dst, device, at_slot=None):
         at_slot = slot() if at_slot is None else at_slot
         i = count[0] % N_SEND
@@ -251,13 +262,13 @@
     def own_x(tag, h):
         rows, cols, far = pl.ds(*HALVES[h][:2]), columns(h, tag), tag in "zy"
         src = b[f"own{tag}{h}"] if far else n_all.at[0, rows, cols]
-        k = slot()
+        k = slot_of(h)
         send(src, n_all.at[3, rows, cols], dev(dx=1), k)
         send(src, n_all.at[1, rows, cols], dev(dx=-1), k)
         cps[tag, h] = k, n_all.at[0:2, rows, cols]
         if far:
             dst = n_all.at[2, rows, cols]
-            cps[tag, h, "far"] = send(src, dst, dev(dx=2)), dst
+            cps[tag, h, "far"] = send(src, dst, dev(dx=2), slot_of(h)), dst
 
     def chain(tag, h, n, axis, rel):
         half = n // 2
@@ -267,14 +278,14 @@
         def begin():
             for sign in (1, -1):
                 ref = n_all.at[rel, full, columns(h, tag)]
-                cps[tag, h, rel, sign, 1] = send(ref, ref, dev(**{axis: sign})), ref
+                cps[tag, h, rel, sign, 1] = send(ref, ref, dev(**{axis: sign}), slot_of(h)), ref
 
         def arrive(sign, k):
             arrived(*cps[tag, h, rel, sign, k])
             if k < half:
                 rows = full if k < half - 1 else (low if sign == 1 else high)
                 ref = n_all.at[rel, rows, columns(h, tag, -sign * k)]
-                cps[tag, h, rel, sign, k + 1] = send(ref, ref, dev(**{axis: sign})), ref
+                cps[tag, h, rel, sign, k + 1] = send(ref, ref, dev(**{axis: sign}), slot_of(h)), ref
 
         for k in range(1, half + 1):
             for sign in (1, -1):
@@ -292,7 +303,7 @@
             rows, cols = pl.ds(*HALVES[h][:2]), columns(h, tag)
             rel, dx = (1, -1) if tag == "b" else (3, 1)
             dst = n_all.at[2, rows, cols]
-            cps[tag, h, 2] = send(n_all.at[rel, rows, cols], dst, dev(dx=dx)), dst
+            cps[tag, h, 2] = send(n_all.at[rel, rows, cols], dst, dev(dx=dx), slot_of(h)), dst
 
         for tag, n, axis in (("z", NZ, "dz"), ("y", NY, "dy")):
             more = [lambda k=k: own_x(*k) for k in AFTER.get((tag, h), ())]
@@ -480,7 +491,7 @@
         def begin(sign):
             for i in range(n_chains):
                 src = one_way(block(half, i), sign)
-                cps[tag, h, sign, 1, i] = send(src, buf_a.at[side[sign], i], dev(**{axis: sign}))
+                cps[tag, h, sign, 1, i] = send(src, buf_a.at[side[sign], i], dev(**{axis: sign}), spare(h))
 
         def arrive(sign, k, i):
             arrived(cps[tag, h, sign, k, i], buf_a.at[side[sign], i] if k == 1 else buf_b.at[side[sign], i, k - 2])
@@ -490,7 +501,7 @@
             else:
                 add_into(block(d, i), [buf_b.at[side[sign], i, k - 2]])
             cps[tag, h, sign, k + 1, i] = send(
-                block(d, i), buf_b.at[side[sign], i, k - 1], dev(**{axis: sign})
+                block(d, i), buf_b.at[side[sign], i, k - 1], dev(**{axis: sign}), spare(h)
             )
 
         def finish(i):
@@ -511,7 +522,7 @@
 
     def direct(tag, h, n, axis, block, buf, done):
         def begin():
-            cps[tag, h] = slot()
+            cps[tag, h] = spare(h)
             for d in range(1, n):
                 send(block(d), buf.at[d - 1], dev(**{axis: d}), cps[tag, h])
 
@@ -529,7 +540,7 @@
         pairs = [(i, j) for i in range(sizes[0]) for j in range(sizes[1]) if i or j]
 
         def begin():
-            cps[tag, h] = slot()
+            cps[tag, h] = spare(h)
             for q, (i, j) in enumerate(pairs):
                 send(block(i, j), buf.at[q], dev(**{axes[0]: i, axes[1]: j}), cps[tag, h])
 

time: 78.1 us -> 77.4 us (level)
  no operation moved by 1% of the time
where the time goes in v7:
time: 77.4 us; the launch traced here: 77.2 us
  Pallas kernels  76.4 us (99%)
  between operations  0.8 us (1%)
    pallas_call x1, Pallas kernels, body(): pl.pallas_call(kernel, out_shape=(jax.ShapeDtypeStruct((1, 1), F32), big,...  72.4 us
    pallas_call x1, Pallas kernels, body(): pl.pallas_call(handover, out_shape=(jax.ShapeDtypeStruct((1, 1), F32), bi...  4.04 us

profile of v7, /device:TPU:2, one launch (start us, length us, event | category | flops | bytes accessed | tf_op | source)
XLA Modules:
  0.0 77.2 jit_solution(1556285641397138192)
XLA Ops:
  0.6 72.4 %exit_head.1 = (f32[1,1]{1,0:T(1,128)}, bf16[8192,256]{1,0:T(8,128)(2,1)}, bf16[80,256]{1,0:T(8,128)(2,1)}) custom-call(bf16[80,8192]{1,0:T(8,128)(2,1)} %hidden.1, f32[4,8192]{1,0:T(4,128)} %gain_in.1, bf16[8192,256]{1,0:T(8,128)(2,1)} %head.1, s32[640]{0:T(1024)} %targets.1, s32[640]{0:T(1024)} %exit_ids.1, s32[8]{0:T(128)} %counts.1, f32[4]{0:T(128)} %scale.1), custom_call_target="tpu_custom_call" | custom-call | tf_op jit(solution)/shard_map/exit_head/pallas_call | solution.py:675
  73.0 4.0 %handover.1 = (f32[1,1]{1,0:T(1,128)}, bf16[8192,256]{1,0:T(8,128)(2,1)}, bf16[80,256]{1,0:T(8,128)(2,1)}) custom-call(f32[1,1]{1,0:T(1,128)} %get-tuple-element.9.loss, bf16[8192,256]{1,0:T(8,128)(2,1)} %get-tuple-element.10.grad_weight, bf16[80,256]{1,0:T(8,128)(2,1)} %get-tuple-element.11.grad_hidden), custom_call_target="tpu_custom_call" | custom-call | tf_op jit(solution)/shard_map/handover/pallas_call | solution.py:686
